TPU v7x, 32 devices: a whole 2x2x4 slice. The times are simulated.
32 devices in a mesh: rng: 8 (over z, x), az: 4 (over y, core).
Axes of the slice: x: 2, y: 2, z: 4, core: 2. Of those that a mesh axis runs over, the one named last changes fastest.
Arguments:
- sar_image: float32 [2, 512, 16384], P(None, 'rng', 'az'), may hold values from -6 to 6
- strong_index: int32 [256], P('rng'), may hold values from 0 to 511, as said below
- shifts: int32 [256], P('rng'), may hold values from 0 to 16383
- widths: int32 [256], P('rng'), may hold values from 256 to 2048
Outputs:
- focused_image: float32 [2, 512, 16384], P(None, 'rng', 'az')
- phase_error: float32 [16384], P('az')
Inputs may be any that keep to these rules, and one draw needn't show every extreme that they name: `strong_index`: entries r * 32 to (r + 1) * 32 - 1 are distinct range bins of the block r * 64 to (r + 1) * 64 - 1.
All inputs are finite; a program needn't handle non-finite values.
Results may differ from a plain program's by a relative error of at most 0.0003.
Values sent between devices are 32-bit elements; how exact they have to be, the bound alone decides.
A program may use at most 64 MiB of HBM per device.

v0:
```python
import math

import jax
import jax.numpy as jnp
from jax import lax
from jax.sharding import PartitionSpec as P

ITERS = 2


epsilon = 1e-06


def make_tables(pulses):
    first = max((factor for factor in range(1, math.isqrt(pulses) + 1) if pulses % factor == 0))
    second = pulses // first

    def table(count_rows, count_cols, modulus):
        product = (
            jnp.arange(count_rows, dtype=jnp.int32)[:, None]
            * jnp.arange(count_cols, dtype=jnp.int32)[None, :]
            % modulus
        )
        angle = -2.0 * math.pi / modulus * product.astype(jnp.float32)
        return (jnp.cos(angle), jnp.sin(angle))

    return (
        first,
        second,
        table(second, second, second),
        table(second, first, pulses),
        table(first, first, first),
    )


def complex_product(real_part, imag_part, matrix, form):

    def single(left, right):
        return jnp.einsum(form, left, right, precision=lax.Precision.HIGHEST)

    return (
        single(real_part, matrix[0]) - single(imag_part, matrix[1]),
        single(real_part, matrix[1]) + single(imag_part, matrix[0]),
    )


def forward(real_part, imag_part, tables):
    first, second, outer, twist, inner = tables
    count = real_part.shape[0]
    pulses = real_part.shape[1]
    section_r, section_i = complex_product(
        real_part.reshape(count, second, first),
        imag_part.reshape(count, second, first),
        outer,
        "rab,ak->rkb",
    )
    turned_r = section_r * twist[0] - section_i * twist[1]
    turned_i = section_r * twist[1] + section_i * twist[0]
    final_r, final_i = complex_product(turned_r, turned_i, inner, "rkb,bj->rjk")
    factor = 1.0 / math.sqrt(pulses)
    return (final_r.reshape(count, pulses) * factor, final_i.reshape(count, pulses) * factor)


def inverse(real_part, imag_part, tables):
    out_r, out_i = forward(real_part, -imag_part, tables)
    return (out_r, -out_i)


def correct(hist_r, hist_i, total):
    cosine = jnp.cos(total)[None, :]
    sine = jnp.sin(total)[None, :]
    return (hist_r * cosine + hist_i * sine, hist_i * cosine - hist_r * sine)


def center_window(real_part, imag_part, line_shift, line_width):
    pulses = real_part.shape[1]
    cells = jnp.arange(pulses, dtype=jnp.int32)
    starts = (line_shift - pulses // 2) % pulses
    lower = pulses // 2 - line_width // 2
    inside = (
        (cells[None, :] >= lower[:, None]) & (cells[None, :] < (lower + line_width)[:, None])
    ).astype(jnp.float32)
    stacked = jnp.stack([real_part, imag_part])
    doubled = jnp.concatenate([stacked, stacked], axis=2)

    def roll_row(row, begin):
        return lax.dynamic_slice_in_dim(row, begin, pulses, 1)

    moved = jax.vmap(roll_row, in_axes=(1, 0), out_axes=1)(doubled, starts)
    return (moved[0] * inside, moved[1] * inside)


def gradient_terms(spec_r, spec_i):
    cross = jnp.sum(spec_r[:, :-1] * spec_i[:, 1:] - spec_i[:, :-1] * spec_r[:, 1:], axis=0)
    numerator = jnp.concatenate([jnp.zeros((1,), jnp.float32), cross])
    denominator = jnp.sum(spec_r * spec_r + spec_i * spec_i, axis=0)
    return (numerator, denominator)


def phase_step(numerator, denominator):
    summed_num, summed_den = lax.psum((numerator, denominator), ("rng", "az"))
    return jnp.cumsum(summed_num / (summed_den + epsilon))


def local(sar_image, strong_index, shifts, widths):
    bins_local = sar_image.shape[1]
    pulses_local = sar_image.shape[2]
    rows = lax.all_to_all(sar_image, "az", split_axis=1, concat_axis=2, tiled=True)
    pulses = rows.shape[2]
    tables = make_tables(pulses)
    hist_r, hist_i = forward(rows[0], rows[1], tables)
    local_strong = strong_index % bins_local
    total = jnp.zeros((pulses,), jnp.float32)
    count = rows.shape[1]
    row_ids = lax.axis_index("az") * count + jnp.arange(count, dtype=jnp.int32)
    matches = (row_ids[:, None] == local_strong[None, :]).astype(jnp.int32)
    line_shift = jnp.sum(matches * shifts[None, :], axis=1)
    line_width = jnp.sum(matches * widths[None, :], axis=1)
    for step in range(ITERS):
        if step == 0:
            lines_r, lines_i = (rows[0], rows[1])
        else:
            lines_r, lines_i = inverse(*correct(hist_r, hist_i, total), tables)
        centered_r, centered_i = center_window(lines_r, lines_i, line_shift, line_width)
        spec_r, spec_i = forward(centered_r, centered_i, tables)
        total = total + phase_step(*gradient_terms(spec_r, spec_i))
    final_r, final_i = inverse(*correct(hist_r, hist_i, total), tables)
    focused_image = lax.all_to_all(
        jnp.stack([final_r, final_i]), "az", split_axis=2, concat_axis=1, tiled=True
    )
    phase_error = lax.dynamic_slice_in_dim(total, lax.axis_index("az") * pulses_local, pulses_local)
    return (focused_image, phase_error)


def solution(mesh):
    placed = (P(None, "rng", "az"), P("rng"), P("rng"), P("rng"))
    return jax.shard_map(
        local,
        mesh=mesh,
        in_specs=placed,
        out_specs=(P(None, "rng", "az"), P("az")),
        check_vma=False,
    )
```

profile of v0, /device:TPU:0, one launch (start us, length us, event | category | flops | bytes accessed | tf_op | source)
XLA Modules:
  0.0 654.8 jit_solution(7235507566148588880)
XLA Ops:
  7.2 4.5 copy.72
  11.7 4.4 all-to-all-start
  17.2 24.6 %all-to-all-done = f32[2,64,4096]{2,0,1:T(2,128)S(1)} async-done(((f32[2,64,4096]{2,0,1:T(2,128)}), f32[2,64,4096]{2,0,1:T(2,128)S(1)}, u32[]{:S(2)}, u32[]{:S(2)}) %all-to-all-start) | async-done | bytes 2097184 | tf_op jit(solution)/shard_map/all_to_all | solution.py:108
  59.6 4.9 maximum_bitcast_fusion
  66.7 57.2 %while.2 = (s32[]{:T(128)}, f32[16,2,32768]{2,1,0:T(2,128)}, s32[16,3]{0,1:T(4,128)S(1)}, f32[16,2,16384]{2,1,0:T(2,128)}, s32[]{:T(128)}) while((s32[]{:T(128)}, f32[16,2,32768]{2,1,0:T(2,128)}, s32[16,3]{0,1:T(4,128)S(1)}, f32[16,2,16384]{2,1,0:T(2,128)}, s32[]{:T(128)}) %tuple.47), condition=%wide.while_cond, body=%wide.while_body.sunk | while | flops 2 | bytes 263285 | solution.py:87
  67.3 3.0 dynamic-slice_dynamic-update-slice_fusion.4
  70.9 3.0 dynamic-slice_dynamic-update-slice_fusion.4
  74.5 3.0 dynamic-slice_dynamic-update-slice_fusion.4
  78.0 3.0 dynamic-slice_dynamic-update-slice_fusion.4
  81.6 3.0 dynamic-slice_dynamic-update-slice_fusion.4
  85.2 3.0 dynamic-slice_dynamic-update-slice_fusion.4
  88.8 3.0 dynamic-slice_dynamic-update-slice_fusion.4
  92.3 3.0 dynamic-slice_dynamic-update-slice_fusion.4
  95.9 3.0 dynamic-slice_dynamic-update-slice_fusion.4
  99.5 3.0 dynamic-slice_dynamic-update-slice_fusion.4
  103.1 3.0 dynamic-slice_dynamic-update-slice_fusion.4
  106.6 3.0 dynamic-slice_dynamic-update-slice_fusion.4
  110.2 3.0 dynamic-slice_dynamic-update-slice_fusion.4
  123.9 4.3 fusion.353
  137.9 12.8 %fusion.11 = f32[128,16,128]{2,0,1:T(8,128)S(1)} fusion(f32[128,16,128]{2,0,1:T(8,128)S(1)} %fusion.50, f32[128,16,128]{2,0,1:T(8,128)S(1)} %convolution_add_fusion.8, f32[128,16,128]{2,0,1:T(8,128)S(1)} %convolution_subtract_fusion.7, f32[128,128]{1,0:T(8,128)S(1)} %copy.75, f32[128,128]{1,0:T(8,128)S(1)} %copy.74), kind=kOutput, calls=%fused_computation.34 | convolution fusion | flops 404193280 | bytes 4325376 | tf_op jit(solution)/shard_map/rkb,bj->rjk/dot_general | solution.py:39
  158.3 121.2 %all-reduce.8.cloned.1.call-done = (f32[16384]{0:T(1024)}, f32[16384]{0:T(1024)}) async-done(((f32[16384]{0:T(1024)}, f32[16384]{0:T(1024)}), (f32[16384]{0:T(1024)}, f32[16384]{0:T(1024)})) %all-reduce.8.cloned.1.call-update) | async-done | bytes 131088 | tf_op jit(solution)/shard_map/psum | solution.py:101
  292.6 4.9 maximum_bitcast_fusion.1
  299.7 57.8 %while.3 = (s32[]{:T(128)}, f32[16,2,32768]{2,1,0:T(2,128)}, s32[16,3]{0,1:T(4,128)S(1)}, f32[16,2,16384]{2,1,0:T(2,128)}, s32[]{:T(128)}) while((s32[]{:T(128)}, f32[16,2,32768]{2,1,0:T(2,128)}, s32[16,3]{0,1:T(4,128)S(1)}, f32[16,2,16384]{2,1,0:T(2,128)}, s32[]{:T(128)}) %tuple.59), condition=%wide.while_cond.1, body=%wide.while_body.1.sunk | while | flops 2 | bytes 263285 | solution.py:87
  300.3 3.0 dynamic-slice_dynamic-update-slice_fusion.5
  304.0 3.0 dynamic-slice_dynamic-update-slice_fusion.5
  307.6 3.0 dynamic-slice_dynamic-update-slice_fusion.5
  311.2 3.0 dynamic-slice_dynamic-update-slice_fusion.5
  314.8 3.0 dynamic-slice_dynamic-update-slice_fusion.5
  318.4 3.0 dynamic-slice_dynamic-update-slice_fusion.5
  322.0 3.0 dynamic-slice_dynamic-update-slice_fusion.5
  325.6 3.0 dynamic-slice_dynamic-update-slice_fusion.5
  329.2 3.0 dynamic-slice_dynamic-update-slice_fusion.5
  332.8 3.0 dynamic-slice_dynamic-update-slice_fusion.5
  336.5 3.0 dynamic-slice_dynamic-update-slice_fusion.5
  340.1 3.0 dynamic-slice_dynamic-update-slice_fusion.5
  343.7 3.0 dynamic-slice_dynamic-update-slice_fusion.5
  347.3 3.0 dynamic-slice_dynamic-update-slice_fusion.5
  350.9 3.0 dynamic-slice_dynamic-update-slice_fusion.5
  354.5 3.0 dynamic-slice_dynamic-update-slice_fusion.5
  357.5 4.4 fusion.352
  376.5 122.0 %all-reduce.6.cloned.1.call-done = (f32[16384]{0:T(1024)}, f32[16384]{0:T(1024)}) async-done(((f32[16384]{0:T(1024)}, f32[16384]{0:T(1024)}), (f32[16384]{0:T(1024)}, f32[16384]{0:T(1024)})) %all-reduce.6.cloned.1.call-update) | async-done | bytes 131088 | tf_op jit(solution)/shard_map/psum | solution.py:101
  519.9 14.8 %copy.87 = f32[2,16,16384]{1,0,2:T(2,128)} copy(f32[2,16,16384]{2,1,0:T(8,128)S(1)} %pad_maximum_fusion) | data formatting | bytes 4194304 | tf_op jit(solution)/shard_map/stack | solution.py:129
  534.7 25.4 %reshape.443 = f32[4,1,131072]{2,1,0:T(1,128)} reshape(f32[16384,2,16]{2,1,0:T(2,128)} %bitcast.233) | data formatting | bytes 4194304
  560.1 4.0 all-to-all-start.1
  564.8 24.5 %all-to-all-done.1 = f32[4,1,131072]{2,1,0:T(1,128)S(1)} async-done(((f32[4,1,131072]{2,1,0:T(1,128)}), f32[4,1,131072]{2,1,0:T(1,128)S(1)}, u32[]{:S(2)}, u32[]{:S(2)}) %all-to-all-start.1) | async-done | bytes 2097184 | tf_op jit(solution)/shard_map/all_to_all | solution.py:128
  591.3 7.8 %reduce.8 = f32[4,131072]{1,0:T(4,128)S(1)} reduce(f32[4,1,131072]{2,1,0:T(1,128)} %copy-done.3, f32[]{:T(128)} %broadcast.794), dimensions={1}, to_apply=%all_to_all.27.reduce_sub_computation | reduce | bytes 4194308 | tf_op jit(solution)/shard_map/all_to_all | solution.py:128
  599.0 28.7 %reshape.444 = f32[16384,2,16]{2,1,0:T(2,128)} reshape(f32[4,131072]{1,0:T(4,128)S(1)} %reduce.8) | data formatting | bytes 4194304
  627.7 20.0 %copy.88 = f32[2,4,16,4096]{3,2,1,0:T(8,128)} copy(f32[2,4,16,4096]{2,0,3,1:T(2,128)} %bitcast.234) | data formatting | bytes 4194304 | tf_op jit(solution)/shard_map/all_to_all | solution.py:128
  (187 shorter events, 120.6 us)
Async XLA Ops:
  11.7 5.2 copy-start.10
  11.7 5.3 copy-start.8
  11.7 5.3 copy-start.9
  11.7 30.1 %all-to-all-start = ((f32[2,64,4096]{2,0,1:T(2,128)}), f32[2,64,4096]{2,0,1:T(2,128)S(1)}, u32[]{:S(2)}, u32[]{:S(2)}) async-start(f32[2,64,4096]{2,0,1:T(2,128)} %copy.72), calls=%async_computation | async-start | bytes 4194304 | tf_op jit(solution)/shard_map/all_to_all | solution.py:108
  16.1 263.4 %all-reduce.8.cloned.1.call-start = ((), (), s32[]{:S(2)}) async-start(), calls=%async_computation.3 | async-start | bytes 262144 | tf_op jit(solution)/shard_map/psum | solution.py:101
  54.7 81.8 %copy-start = (f32[128,16,128]{2,0,1:T(8,128)}, f32[128,16,128]{2,0,1:T(8,128)S(1)}, u32[]{:S(2)}) copy-start(f32[128,16,128]{2,0,1:T(8,128)S(1)} %convolution_subtract_fusion.9) | copy-start | bytes 3145732
  57.3 2.3 copy-start.5
  57.3 2.3 copy-start.6
  135.2 1.3 copy-start.4
  155.4 343.1 %all-reduce.6.cloned.1.call-start = ((), (), s32[]{:S(2)}) async-start(), calls=%async_computation.2 | async-start | bytes 262144 | tf_op jit(solution)/shard_map/psum | solution.py:101
  506.1 2.6 copy-start.1
  511.2 2.5 copy-start.2
  516.0 2.5 copy-start.7
  560.1 29.3 %all-to-all-start.1 = ((f32[4,1,131072]{2,1,0:T(1,128)}), f32[4,1,131072]{2,1,0:T(1,128)S(1)}, u32[]{:S(2)}, u32[]{:S(2)}) async-start(f32[4,1,131072]{2,1,0:T(1,128)} %reshape.443), calls=%async_computation.1 | async-start | bytes 4194304 | tf_op jit(solution)/shard_map/all_to_all | solution.py:128
  589.4 1.3 copy-start.3
Sparse Core Ops, SparseCore 0:
  155.5 123.9 all-reduce.7
  376.6 121.7 all-reduce.5
where the time goes:
time: 667 us; the launch traced here: 655 us
  waiting for transfers between devices  292 us (44%)
  local copies, waits for them, and re-layouts  241 us (36%)
  matrix products  73.1 us (11%)
  other arithmetic  25.5 us (4%)
  between operations  14.8 us (2%)
  starting transfers between devices  8.43 us (1%)
    psum x2, waiting for transfers between devices, phase_step(): summed_num, summed_den = lax.psum((numerator, denominator), ('rng', 'az'))  243 us
    gather x96, local copies, waits for them, and re-layouts  115 us
    dot_general x40, matrix products, single(): return jnp.einsum(form, left, right, precision=lax.Precision.HIGHEST)  73.1 us
    unnamed x30, local copies, waits for them, and re-layouts  65.5 us
    all_to_all x1, waiting for transfers between devices, local(): lax.all_to_all(sar_image, 'az', split_axis=1, concat_axis=2, tiled=True)  24.6 us
    all_to_all x1, waiting for transfers between devices, local(): lax.all_to_all(jnp.stack([final_r, final_i]), 'az', split_axis=2, concat_...  24.5 us
    all_to_all x2, local copies, waits for them, and re-layouts, local(): lax.all_to_all(jnp.stack([final_r, final_i]), 'az', split_axis=2, concat_...  20.6 us
    another operation x1, local copies, waits for them, and re-layouts, local(): jnp.stack([final_r, final_i])  14.8 us
  transfers between devices with their start and end apart: 4, of which 4 were waited for; matrix products, arithmetic and copies ran while one was open for 1% of the time, Pallas kernels for 0%

commit v1 on v0

v1 whole, which is shorter than its diff:
```python
import functools
import math

import jax
import jax.numpy as jnp
import ml_dtypes
import numpy as np
from jax import lax
from jax.experimental import pallas as pl
from jax.experimental.pallas import tpu as pltpu
from jax.sharding import PartitionSpec as P

ITERS = 2
SIDE = 128
MESH = pl.DeviceIdType.MESH

epsilon = 1e-06


def split(value):
    high = value.astype(ml_dtypes.bfloat16)
    low = (value - high.astype(np.float64)).astype(ml_dtypes.bfloat16)
    return high, low


def make_tables():
    pulses = SIDE * SIDE
    grid = np.arange(SIDE)[:, None] * np.arange(SIDE)[None, :]
    angle = 2.0 * math.pi / SIDE * (grid % SIDE)
    cosine, sine = np.cos(angle), np.sin(angle)
    ahead = np.block([[cosine, sine], [-sine, cosine]])
    back = np.block([[cosine, -sine], [sine, cosine]])
    ahead_h, ahead_l = split(ahead)
    back_h, back_l = split(back)
    turn = 2.0 * math.pi / pulses * grid
    twist = np.stack([np.tile(np.cos(turn), (1, 2)), np.tile(np.sin(turn), (1, 2))]) / SIDE
    return (
        np.concatenate([ahead_h, ahead_l, ahead_h], axis=1),
        np.concatenate([back_h, back_h, back_l], axis=0),
        np.concatenate([ahead_h, ahead_h, ahead_l], axis=0),
        np.concatenate([back_h, back_l, back_h], axis=1),
        twist.astype(np.float32),
    )


def make_turns():
    units = np.arange(SIDE)
    coarse = 2.0 * math.pi / SIDE * units
    fine = 2.0 * math.pi / (SIDE * SIDE) * units
    columns = []
    for exact in (-np.cos(coarse), -np.sin(coarse), np.cos(fine), np.sin(fine)):
        high = np.round(exact * 2048.0) / 2048.0
        columns += [high, exact - high]
    return np.concatenate(columns).astype(np.float32)


def line_turn(turns, shift):
    coarse, fine = shift // SIDE, shift % SIDE
    cc_h, cc_l, cs_h, cs_l = [turns[coarse + SIDE * at] for at in range(4)]
    fc_h, fc_l, fs_h, fs_l = [turns[fine + SIDE * at] for at in range(4, 8)]
    cos_h = cc_h * fc_h - cs_h * fs_h
    cos_l = (cc_h * fc_l + cc_l * (fc_h + fc_l)) - (cs_h * fs_l + cs_l * (fs_h + fs_l))
    sin_h = cs_h * fc_h + cc_h * fs_h
    sin_l = (cs_h * fc_l + cs_l * (fc_h + fc_l)) + (cc_h * fs_l + cc_l * (fs_h + fs_l))
    return cos_h, cos_l, sin_h, sin_l


def halves(value):
    high = value.astype(jnp.bfloat16)
    low = (value - high.astype(jnp.float32)).astype(jnp.bfloat16)
    return high, low


def left(matrix_ref, value):
    high, low = halves(value)
    stacked = jnp.concatenate([high, high, low], axis=0)
    return jnp.dot(matrix_ref[...], stacked, preferred_element_type=jnp.float32)


def right(value, matrix_ref):
    high, low = halves(value)
    stacked = jnp.concatenate([high, low, high], axis=1)
    return jnp.dot(stacked, matrix_ref[...], preferred_element_type=jnp.float32)


def lanes_to_rows(real_part, imag_part):
    return jnp.concatenate(
        [
            jnp.concatenate([real_part[:, :SIDE], imag_part[:, :SIDE]], axis=1),
            jnp.concatenate([real_part[:, SIDE:], imag_part[:, SIDE:]], axis=1),
        ],
        axis=0,
    )


def rows_to_lanes(value):
    real_part = jnp.concatenate([value[:SIDE, :SIDE], value[SIDE:, :SIDE]], axis=1)
    imag_part = jnp.concatenate([value[:SIDE, SIDE:], value[SIDE:, SIDE:]], axis=1)
    return real_part, imag_part


def forward(pair, ahead_left, back_right, twist):
    section = left(ahead_left, pair)
    sec_r, sec_i = section[:SIDE], section[SIDE:]
    cosine, sine = twist[0], twist[1]
    turned = lanes_to_rows(sec_r * cosine + sec_i * sine, sec_i * cosine - sec_r * sine)
    return right(turned, back_right)


def inverse(spectrum, ahead_right, back_left, twist):
    sec_r, sec_i = rows_to_lanes(right(spectrum, ahead_right))
    cosine, sine = twist[0], twist[1]
    turned = jnp.concatenate(
        [sec_r * cosine - sec_i * sine, sec_i * cosine + sec_r * sine], axis=0
    )
    return left(back_left, turned)


def correct(spectrum, cosine, sine):
    rows = []
    for line in range(2):
        part = spectrum[line * SIDE : (line + 1) * SIDE]
        real_part, imag_part = part[:, :SIDE], part[:, SIDE:]
        rows.append(
            jnp.concatenate(
                [real_part * cosine + imag_part * sine, imag_part * cosine - real_part * sine],
                axis=1,
            )
        )
    return jnp.concatenate(rows, axis=0)


def previous(value):
    down = pltpu.roll(value, 1, 0)
    top = down[:8]
    wrapped = pltpu.roll(top, 1, 1)
    first = lax.broadcasted_iota(jnp.int32, (8, SIDE), 0) == 0
    return jnp.concatenate([jnp.where(first, wrapped, top), down[8:]], axis=0)


def kernel(
    ranks,
    parts,
    strong,
    sar_hbm,
    places,
    turns,
    ahead_left_hbm,
    back_right_hbm,
    ahead_right_hbm,
    back_left_hbm,
    twist_hbm,
    image_hbm,
    phase_out,
    sar,
    ahead_left,
    back_right,
    ahead_right,
    back_left,
    twist,
    plain,
    stage,
    rows,
    hist,
    sums,
    phase,
    sums_out,
    sums_in,
    grads,
    ready,
    landed,
    image,
    load_sem,
    image_sem,
    in_send,
    in_recv,
    sum_send,
    sum_recv,
    grad_send,
    grad_recv,
    out_send,
    out_recv,
):
    devices = ranks * parts
    reducers = sums_out.shape[1]
    block = SIDE // reducers
    rank = lax.axis_index("rng")
    part = lax.axis_index("az")
    me = rank * parts + part
    lines = rows.shape[1]
    pairs = lines // 2
    bins = stage.shape[1]
    depth = stage.shape[2]
    mine_strong = strong // parts
    mine_other = lines - mine_strong
    strong_pairs = mine_strong // 2
    groups = bins // 8
    slot_at, bin_at, shift_at, width_at = 0, bins, 2 * bins, 2 * bins + strong

    loads = [
        pltpu.make_async_copy(source, target, load_sem.at[at])
        for at, (source, target) in enumerate(
            [
                (sar_hbm, sar),
                (ahead_left_hbm, ahead_left),
                (twist_hbm, twist),
                (back_right_hbm, back_right),
                (ahead_right_hbm, ahead_right),
                (back_left_hbm, back_left),
            ]
        )
    ]
    loads[0].start()

    barrier = pltpu.get_barrier_semaphore()

    @pl.loop(1, devices)
    def _(step):
        other = (me + step) % devices
        pl.semaphore_signal(
            barrier, inc=1, device_id=(other // parts, other % parts), device_id_type=MESH
        )

    for load in loads[1:]:
        load.start()
    loads[0].wait()

    for half in range(2):

        @pl.loop(0, groups)
        def _(group):
            spot = pl.ds(pl.multiple_of(group * 8, 8), 8)
            plain[half, spot] = sar[half, spot, :].reshape(8, depth, SIDE)

    def arrange(first, last):
        @pl.loop(first, last)
        def _(slot):
            source = places[bin_at + slot]
            for half in range(2):
                stage[half, slot] = plain[half, source]

    arrange(0, strong)
    pl.semaphore_wait(barrier, devices - 1)

    mine = pl.ds(pl.multiple_of(part * depth, depth), depth)

    def strong_slot(pair, owner):
        return mine_strong * owner + 2 * pair

    def other_slot(pair, owner):
        return strong + mine_other * owner + 2 * (pair - strong_pairs)

    def bring(slot_of, pair, source, target):
        return pltpu.make_async_remote_copy(
            src_ref=stage.at[:, pl.ds(slot_of(pair, target), 2)],
            dst_ref=rows.at[:, pl.ds(2 * pair, 2), pl.ds(pl.multiple_of(source * depth, depth), depth)],
            send_sem=in_send.at[pair, target],
            recv_sem=in_recv.at[pair, source],
            device_id=(rank, target),
            device_id_type=MESH,
        )

    order = sorted(range(1, parts), key=lambda step: abs(step - parts // 2))

    def begin(slot_of, pair):
        for step in order:
            bring(slot_of, pair, part, (part + step) % parts).start()

    def arrived(slot_of, pair):
        for step in order:
            other = (part + step) % parts
            bring(slot_of, pair, other, other).wait_recv()

    @pl.loop(0, strong_pairs)
    def _(pair):
        begin(strong_slot, pair)

    arrange(strong, bins)
    for half in range(2):

        @pl.loop(0, mine_strong)
        def _(line):
            rows[half, line, mine, :] = stage[half, mine_strong * part + line]

        @pl.loop(0, mine_other)
        def _(line):
            rows[half, mine_strong + line, mine, :] = stage[half, strong + mine_other * part + line]

    sums[...] = jnp.zeros_like(sums)
    cells = (
        lax.broadcasted_iota(jnp.int32, (SIDE, SIDE), 0) * SIDE
        + lax.broadcasted_iota(jnp.int32, (SIDE, SIDE), 1)
    )
    for load in loads[1:]:
        load.wait()

    def add_terms(pair, value):
        masks = []
        for line in range(2):
            at = mine_strong * part + pair * 2 + line
            width = places[width_at + at]
            offset = (cells - (places[shift_at + at] - width // 2)) & (SIDE * SIDE - 1)
            masks.append((offset < width).astype(jnp.float32))
        mask = jnp.concatenate(masks, axis=1)
        mask = jnp.concatenate([mask, mask], axis=0)
        spectra = forward(value * mask, ahead_left, back_right, twist)
        num = sums[0]
        den = sums[1]
        for line in range(2):
            at = mine_strong * part + pair * 2 + line
            cos_h, cos_l, sin_h, sin_l = line_turn(turns, places[shift_at + at])
            spec_r = spectra[line * SIDE : (line + 1) * SIDE, :SIDE]
            spec_i = spectra[line * SIDE : (line + 1) * SIDE, SIDE:]
            prev_r, prev_i = previous(spec_r), previous(spec_i)
            cross_i = prev_r * spec_i - prev_i * spec_r
            cross_r = prev_r * spec_r + prev_i * spec_i
            rest = cross_i * cos_l + cross_r * sin_l
            num = num + ((cross_i * cos_h + cross_r * sin_h) + rest)
            den = den + (spec_r * spec_r + spec_i * spec_i)
        sums[0] = num
        sums[1] = den

    def gathered(pair):
        return jnp.concatenate(
            [
                jnp.concatenate([rows[half, pair * 2], rows[half, pair * 2 + 1]], axis=1)
                for half in range(2)
            ],
            axis=0,
        )

    @pl.loop(0, strong_pairs)
    def _(pair):
        arrived(strong_slot, pair)
        if pairs == 2 * strong_pairs:
            begin(other_slot, strong_pairs + pair)
        value = gathered(pair)
        hist[pair] = forward(value, ahead_left, back_right, twist)
        add_terms(pair, value)

    if pairs != 2 * strong_pairs:

        @pl.loop(strong_pairs, pairs)
        def _(pair):
            begin(other_slot, pair)

    def rest_of_history(first, last):
        @pl.loop(first, last)
        def _(pair):
            arrived(other_slot, pair)
            hist[pair] = forward(gathered(pair), ahead_left, back_right, twist)

    eight_rows = lax.broadcasted_iota(jnp.int32, (8, SIDE), 0)
    row_ids = lax.broadcasted_iota(jnp.int32, (SIDE, SIDE), 0)
    col_ids = lax.broadcasted_iota(jnp.int32, (SIDE, SIDE), 1)

    def reduce_sums(turn, before, after):
        for owner in range(reducers):
            sums_out[turn, owner, :block, :] = sums[0, owner * block : (owner + 1) * block, :]
            sums_out[turn, owner, block:, :] = sums[1, owner * block : (owner + 1) * block, :]

        def give(source, target):
            return pltpu.make_async_remote_copy(
                src_ref=sums_out.at[turn, target],
                dst_ref=sums_in.at[turn, source],
                send_sem=sum_send.at[turn, target],
                recv_sem=sum_recv.at[turn, source],
                device_id=(target // parts, target % parts),
                device_id_type=MESH,
            )

        def share(source, target):
            return pltpu.make_async_remote_copy(
                src_ref=grads.at[turn, source],
                dst_ref=grads.at[turn, source],
                send_sem=grad_send.at[turn, target],
                recv_sem=grad_recv.at[turn, source],
                device_id=(target // parts, target % parts),
                device_id_type=MESH,
            )

        def each_other(count, act):
            if count == devices:

                @pl.loop(1, devices)
                def _(step):
                    act((me + step) % devices)

            else:

                @pl.loop(0, count)
                def _(other):
                    @pl.when(other != me)
                    def _():
                        act(other)

        def reducing(act):
            if reducers == devices:
                act()
            else:
                pl.when(me < reducers)(act)

        each_other(reducers, lambda other: give(me, other).start())

        before()

        def combine():
            def add(step, total):
                other = (me + step) % devices
                give(other, me).wait_recv()
                return total + sums_in[turn, other]

            total = lax.fori_loop(1, devices, add, sums_out[turn, me])
            swapped = pltpu.roll(total, block, 0)
            upper = eight_rows < block
            num = jnp.where(upper, total, swapped)
            den = jnp.where(upper, swapped, total)
            no_first = (
                (eight_rows % block == 0)
                & (lax.broadcasted_iota(jnp.int32, (8, SIDE), 1) == 0)
                & (me == 0)
            )
            grads[turn, me] = jnp.where(no_first, 0.0, num / (den + epsilon))
            each_other(devices, lambda other: share(me, other).start())

        reducing(combine)
        after()
        each_other(reducers, lambda other: share(other, other).wait_recv())
        tiles = [
            jnp.where(eight_rows < block, grads[turn, 2 * at], grads[turn, 2 * at + 1])
            for at in range(reducers // 2)
        ]
        gradient = jnp.concatenate(tiles, axis=0)
        lower = (row_ids >= col_ids).astype(jnp.float32)
        upper = (row_ids < col_ids).astype(jnp.float32)
        inside = jnp.dot(
            lower, gradient, precision=lax.Precision.HIGHEST, preferred_element_type=jnp.float32
        )
        columns = jnp.broadcast_to(inside[SIDE - 1 :], (8, SIDE))
        before = jnp.dot(
            columns, upper, precision=lax.Precision.HIGHEST, preferred_element_type=jnp.float32
        )
        running = inside + before[:1]
        phase[...] = running if turn == 0 else phase[...] + running
        each_other(reducers, lambda other: give(me, other).wait_send())

        def drain():
            each_other(devices, lambda other: share(me, other).wait_send())

        reducing(drain)

    def nothing():
        pass

    halfway = strong_pairs + (pairs - strong_pairs) // 2
    reduce_sums(0, nothing, nothing)
    for turn in range(1, ITERS):
        cosine, sine = jnp.cos(phase[...]), jnp.sin(phase[...])
        sums[...] = jnp.zeros_like(sums)

        @pl.loop(0, strong_pairs)
        def _(pair):
            add_terms(
                pair, inverse(correct(hist[pair], cosine, sine), ahead_right, back_left, twist)
            )

        if turn == ITERS - 1:
            reduce_sums(
                turn,
                lambda: rest_of_history(strong_pairs, halfway),
                lambda: rest_of_history(halfway, pairs),
            )
        else:
            reduce_sums(turn, nothing, nothing)

    cosine, sine = jnp.cos(phase[...]), jnp.sin(phase[...])

    def send_out(slot_of, pair, source, target):
        return pltpu.make_async_remote_copy(
            src_ref=ready.at[:, pl.ds(2 * pair, 2), pl.ds(pl.multiple_of(target * depth, depth), depth)],
            dst_ref=landed.at[:, pl.ds(slot_of(pair, source), 2)],
            send_sem=out_send.at[pair, target],
            recv_sem=out_recv.at[pair, source],
            device_id=(rank, target),
            device_id_type=MESH,
        )

    kinds = ((0, strong_pairs, strong_slot), (strong_pairs, pairs, other_slot))
    for first, last, slot_of in kinds:

        @pl.loop(first, last)
        def _(pair):
            value = inverse(correct(hist[pair], cosine, sine), ahead_right, back_left, twist)
            for half in range(2):
                for line in range(2):
                    ready[half, 2 * pair + line] = value[
                        half * SIDE : (half + 1) * SIDE, line * SIDE : (line + 1) * SIDE
                    ]
            for step in order:
                send_out(slot_of, pair, part, (part + step) % parts).start()
            for half in range(2):
                for line in range(2):
                    landed[half, slot_of(pair, part) + line] = ready[half, 2 * pair + line, mine, :]

    plain[0, : SIDE // depth] = phase[...].T.reshape(SIDE // depth, depth, SIDE)
    phase_out[...] = plain[0, part]

    for first, last, slot_of in kinds:

        @pl.loop(first, last)
        def _(pair):
            for step in order:
                bring(slot_of, pair, part, (part + step) % parts).wait_send()
            for step in order:
                other = (part + step) % parts
                send_out(slot_of, pair, other, other).wait_recv()

    def write(half, group):
        spot = pl.ds(pl.multiple_of(group * 8, 8), 8)
        return pltpu.make_async_copy(
            image.at[half, spot], image_hbm.at[half, spot], image_sem.at[half, group]
        )

    for half in range(2):

        @pl.loop(0, groups)
        def _(group):
            found = [landed[half, places[slot_at + group * 8 + at]] for at in range(8)]
            spot = pl.ds(pl.multiple_of(group * 8, 8), 8)
            image[half, spot, :] = jnp.stack(found).reshape(8, depth * SIDE)
            write(half, group).start()

    for first, last, slot_of in kinds:

        @pl.loop(first, last)
        def _(pair):
            for step in order:
                send_out(slot_of, pair, part, (part + step) % parts).wait_send()

    for half in range(2):

        @pl.loop(0, groups)
        def _(group):
            write(half, group).wait()


def local(ranks, parts, sar_image, strong_index, shifts, widths):
    bins = sar_image.shape[1]
    here = sar_image.shape[2]
    depth = here // SIDE
    lines = bins // parts
    pairs = lines // 2
    strong = strong_index.shape[0]
    devices = ranks * parts
    reducers = min(devices, SIDE // 4)
    chosen = strong_index % bins
    ids = jnp.arange(bins, dtype=jnp.int32)
    same = chosen[None, :] == ids[:, None]
    ahead = (chosen[None, :] < ids[:, None]).astype(jnp.int32)
    order = jnp.arange(strong, dtype=jnp.int32)[None, :]
    is_strong = jnp.any(same, axis=1)
    slots = jnp.where(
        is_strong,
        jnp.sum(jnp.where(same, order, 0), axis=1),
        strong + ids - jnp.sum(ahead, axis=1),
    )
    located = jnp.sum(jnp.where(slots[None, :] == ids[:, None], ids[None, :], 0), axis=1)
    places = jnp.concatenate([slots, located, shifts, widths])
    tables = make_tables()
    vmem = pl.BlockSpec(memory_space=pltpu.VMEM)
    smem = pl.BlockSpec(memory_space=pltpu.SMEM)
    anywhere = pl.BlockSpec(memory_space=pl.ANY)
    dma = pltpu.SemaphoreType.DMA
    image, phase = pl.pallas_call(
        functools.partial(kernel, ranks, parts, strong),
        out_shape=(
            jax.ShapeDtypeStruct((2, bins, here), jnp.float32),
            jax.ShapeDtypeStruct((depth, SIDE), jnp.float32),
        ),
        in_specs=[anywhere, smem, smem] + [anywhere] * 5,
        out_specs=(anywhere, vmem),
        scratch_shapes=[
            pltpu.VMEM((2, bins, here), jnp.float32),
            pltpu.VMEM(tables[0].shape, jnp.bfloat16),
            pltpu.VMEM(tables[1].shape, jnp.bfloat16),
            pltpu.VMEM(tables[2].shape, jnp.bfloat16),
            pltpu.VMEM(tables[3].shape, jnp.bfloat16),
            pltpu.VMEM(tables[4].shape, jnp.float32),
            pltpu.VMEM((2, bins, depth, SIDE), jnp.float32),
            pltpu.VMEM((2, bins, depth, SIDE), jnp.float32),
            pltpu.VMEM((2, lines, SIDE, SIDE), jnp.float32),
            pltpu.VMEM((pairs, 2 * SIDE, 2 * SIDE), jnp.float32),
            pltpu.VMEM((2, SIDE, SIDE), jnp.float32),
            pltpu.VMEM((SIDE, SIDE), jnp.float32),
            pltpu.VMEM((ITERS, reducers, 8, SIDE), jnp.float32),
            pltpu.VMEM((ITERS, devices, 8, SIDE), jnp.float32),
            pltpu.VMEM((ITERS, reducers, 8, SIDE), jnp.float32),
            pltpu.VMEM((2, lines, SIDE, SIDE), jnp.float32),
            pltpu.VMEM((2, bins, depth, SIDE), jnp.float32),
            pltpu.VMEM((2, bins, here), jnp.float32),
            dma((6,)),
            dma((2, bins // 8)),
            dma((pairs, parts)),
            dma((pairs, parts)),
            dma((ITERS, reducers)),
            dma((ITERS, devices)),
            dma((ITERS, devices)),
            dma((ITERS, reducers)),
            dma((pairs, parts)),
            dma((pairs, parts)),
        ],
        compiler_params=pltpu.CompilerParams(
            collective_id=0, has_side_effects=True, vmem_limit_bytes=40 * 2**20
        ),
        name="autofocus",
    )(sar_image, places, jnp.asarray(make_turns()), *[jnp.asarray(t) for t in tables])
    return image, phase.reshape(here)


def solution(mesh):
    placed = (P(None, "rng", "az"), P("rng"), P("rng"), P("rng"))
    return jax.shard_map(
        functools.partial(local, mesh.shape["rng"], mesh.shape["az"]),
        mesh=mesh,
        in_specs=placed,
        out_specs=(P(None, "rng", "az"), P("az")),
        check_vma=False,
    )
```

time: 667 us -> 102 us (0.15); the launches traced: 655 us -> 102 us
  waiting for transfers between devices: 292 us -> 0 us
  local copies, waits for them, and re-layouts: 241 us -> 9.14 us
  Pallas kernels: 0 us -> 90.3 us
  matrix products: 73.1 us -> 0 us
  other arithmetic: 25.5 us -> 1.72 us
  between operations: 14.8 us -> 0.65 us
  starting transfers between devices: 8.43 us -> 0 us
    psum x2 -> x0, waiting for transfers between devices: 243 us -> none  [phase_step(): summed_num, summed_den = lax.psum((numerator, denominator), ('rng', 'az'))]
    gather x96 -> x0, local copies, waits for them, and re-layouts: 115 us -> none
    pallas_call x0 -> x1, Pallas kernels: none -> 90.3 us  [local(): pl.pallas_call(functools.partial(kernel, ranks, parts, strong), out_shape...]
    dot_general x40 -> x0, matrix products: 73.1 us -> none  [single(): return jnp.einsum(form, left, right, precision=lax.Precision.HIGHEST)]
    unnamed x30 -> x16, local copies, waits for them, and re-layouts: 65.5 us -> 9.14 us
    all_to_all x2 -> x0, waiting for transfers between devices: 49.1 us -> none  [the longest x1 24.6 us: local(): lax.all_to_all(sar_image, 'az', split_axis=1, concat_axis=2, tiled=True)]
    all_to_all x3 -> x0, local copies, waits for them, and re-layouts: 22 us -> none  [the longest x2 20.6 us: local(): lax.all_to_all(jnp.stack([final_r, final_i]), 'az', split_axis=2, concat_...]
    another operation x8 -> x0, local copies, waits for them, and re-layouts: 16.7 us -> none  [the longest x1 14.8 us: local(): jnp.stack([final_r, final_i])]
  transfers between devices with their start and end apart: 4 -> 0, of which waited for: 4 -> 0; matrix products, arithmetic and copies ran while one was open for 1% -> 0% of each run, Pallas kernels for 0% -> 0%
where the time goes in v1:
time: 102 us
  Pallas kernels  90.3 us (89%)
  local copies, waits for them, and re-layouts  9.14 us (9%)
  other arithmetic  1.72 us (2%)
    pallas_call x1, Pallas kernels, local(): pl.pallas_call(functools.partial(kernel, ranks, parts, strong), out_shape...  90.3 us
    unnamed x16, local copies, waits for them, and re-layouts  9.14 us

profile of v1, /device:TPU:0, one launch (start us, length us, event | category | flops | bytes accessed | tf_op | source)
XLA Modules:
  0.0 101.8 jit_solution(17307615555585986864)
XLA Ops:
  0.6 0.7 and_select_fusion
  1.3 0.1 fusion
  1.4 0.1 convert_reduce_fusion
  1.5 0.1 select_reduce_fusion
  1.6 0.8 pad_add_fusion.places
  2.4 0.0 copy-start
  2.4 1.6 %copy-done = f32[2,64,4096]{2,1,0:T(8,128)S(1)} copy-done((f32[2,64,4096]{2,1,0:T(8,128)S(1)}, f32[2,64,4096]{2,1,0:T(8,128)}, u32[]{:S(2)}) %copy-start) | copy-done | bytes 2097176
  3.9 0.0 copy-start.1
  3.9 1.0 copy-done.1
  4.9 0.0 copy-start.2
  4.9 1.0 copy-done.2
  5.9 0.0 copy-start.3
  5.9 1.0 copy-done.3
  6.9 0.0 copy-start.4
  6.9 1.0 copy-done.4
  7.9 0.0 copy-start.5
  7.9 0.9 copy-done.5
  8.9 0.0 copy-start.6
  8.9 0.7 copy-done.6
  9.6 90.3 %autofocus.1 = (f32[2,64,4096]{2,1,0:T(8,128)S(1)}, f32[32,128]{1,0:T(8,128)S(1)}) custom-call(f32[2,64,4096]{2,1,0:T(8,128)S(1)} %copy-done, s32[192]{0:T(256)S(1)} %pad_add_fusion.places, f32[1024]{0:T(1024)S(1)} %copy-done.6, bf16[256,768]{1,0:T(8,128)(2,1)S(1)} %copy-done.4, bf16[768,256]{1,0:T(8,128)(2,1)S(1)} %copy-done.3, ...), custom_call_target="tpu_custom_call" | custom-call | tf_op jit(solution)/shard_map/autofocus/pallas_call | solution.py:574
  99.8 1.3 %copy.14 = f32[2,64,4096]{2,1,0:T(8,128)} copy(f32[2,64,4096]{2,1,0:T(8,128)S(1)} %get-tuple-element.10) | data formatting | bytes 4194304
  101.2 0.6 copy.15
  (1 shorter events, 0.0 us)
Async XLA Ops:
  2.4 1.6 %copy-start = (f32[2,64,4096]{2,1,0:T(8,128)S(1)}, f32[2,64,4096]{2,1,0:T(8,128)}, u32[]{:S(2)}) copy-start(f32[2,64,4096]{2,1,0:T(8,128)} %sar_hbm.1) | copy-start | bytes 6291460
  3.9 1.0 copy-start.1
  4.9 1.0 copy-start.2
  5.9 1.0 copy-start.3
  6.9 1.0 copy-start.4
  7.9 0.9 copy-start.5
  8.9 0.7 copy-start.6

commit v2 on v1

v2 whole, which is shorter than its diff:
```python
import functools
import math

import jax
import jax.numpy as jnp
import numpy as np
from jax import lax
from jax.experimental import pallas as pl
from jax.experimental.pallas import tpu as pltpu
from jax.sharding import PartitionSpec as P

ITERS = 2
SIDE = 128
MESH = pl.DeviceIdType.MESH

epsilon = 1e-06


def make_tables(unit):
    pulses = SIDE * SIDE
    grid = np.arange(SIDE)[:, None] * np.arange(SIDE)[None, :]
    angle = 2.0 * math.pi / SIDE * (grid % SIDE)
    cosine, sine = np.cos(angle), np.sin(angle)
    ahead = np.block([[cosine, sine], [-sine, cosine]])
    back = np.block([[cosine, -sine], [sine, cosine]])
    turn = 2.0 * math.pi / pulses * grid
    twist = np.stack([np.tile(np.cos(turn), (1, unit)), np.tile(np.sin(turn), (1, unit))]) / SIDE
    return np.stack([ahead, back]).astype(np.float32), twist.astype(np.float32)


def make_turns():
    units = np.arange(SIDE)
    coarse = 2.0 * math.pi / SIDE * units
    fine = 2.0 * math.pi / (SIDE * SIDE) * units
    columns = []
    for exact in (-np.cos(coarse), -np.sin(coarse), np.cos(fine), np.sin(fine)):
        high = np.round(exact * 2048.0) / 2048.0
        columns += [high, exact - high]
    return np.concatenate(columns).astype(np.float32)


def line_turn(turns, shift):
    coarse, fine = shift // SIDE, shift % SIDE
    cc_h, cc_l, cs_h, cs_l = [turns[coarse + SIDE * at] for at in range(4)]
    fc_h, fc_l, fs_h, fs_l = [turns[fine + SIDE * at] for at in range(4, 8)]
    cos_h = cc_h * fc_h - cs_h * fs_h
    cos_l = (cc_h * fc_l + cc_l * (fc_h + fc_l)) - (cs_h * fs_l + cs_l * (fs_h + fs_l))
    sin_h = cs_h * fc_h + cc_h * fs_h
    sin_l = (cs_h * fc_l + cs_l * (fc_h + fc_l)) + (cc_h * fs_l + cc_l * (fs_h + fs_l))
    return cos_h, cos_l, sin_h, sin_l


def halves(value):
    high = value.astype(jnp.bfloat16)
    low = (value - high.astype(jnp.float32)).astype(jnp.bfloat16)
    return high, low


def left(matrix_ref, value):
    high, low = halves(value)
    stacked = jnp.concatenate([high, high, low], axis=0)
    return jnp.dot(matrix_ref[...], stacked, preferred_element_type=jnp.float32)


def right(value, matrix_ref):
    high, low = halves(value)
    stacked = jnp.concatenate([high, low, high], axis=1)
    return jnp.dot(stacked, matrix_ref[...], preferred_element_type=jnp.float32)


def lanes_to_rows(real_part, imag_part):
    lines = real_part.shape[1] // SIDE
    spots = [slice(line * SIDE, (line + 1) * SIDE) for line in range(lines)]
    return jnp.concatenate(
        [jnp.concatenate([real_part[:, at], imag_part[:, at]], axis=1) for at in spots], axis=0
    )


def rows_to_lanes(value):
    lines = value.shape[0] // SIDE
    spots = [slice(line * SIDE, (line + 1) * SIDE) for line in range(lines)]
    real_part = jnp.concatenate([value[at, :SIDE] for at in spots], axis=1)
    imag_part = jnp.concatenate([value[at, SIDE:] for at in spots], axis=1)
    return real_part, imag_part


def forward(pair, ahead_left, back_right, twist):
    section = left(ahead_left, pair)
    sec_r, sec_i = section[:SIDE], section[SIDE:]
    cosine, sine = twist[0], twist[1]
    turned = lanes_to_rows(sec_r * cosine + sec_i * sine, sec_i * cosine - sec_r * sine)
    return right(turned, back_right)


def inverse(spectrum, ahead_right, back_left, twist):
    sec_r, sec_i = rows_to_lanes(right(spectrum, ahead_right))
    cosine, sine = twist[0], twist[1]
    turned = jnp.concatenate(
        [sec_r * cosine - sec_i * sine, sec_i * cosine + sec_r * sine], axis=0
    )
    return left(back_left, turned)


def correct(spectrum, cosine, sine):
    rows = []
    for line in range(spectrum.shape[0] // SIDE):
        part = spectrum[line * SIDE : (line + 1) * SIDE]
        real_part, imag_part = part[:, :SIDE], part[:, SIDE:]
        rows.append(
            jnp.concatenate(
                [real_part * cosine + imag_part * sine, imag_part * cosine - real_part * sine],
                axis=1,
            )
        )
    return jnp.concatenate(rows, axis=0)


def previous(value):
    down = pltpu.roll(value, 1, 0)
    top = down[:8]
    wrapped = pltpu.roll(top, 1, 1)
    first = lax.broadcasted_iota(jnp.int32, (8, SIDE), 0) == 0
    return jnp.concatenate([jnp.where(first, wrapped, top), down[8:]], axis=0)


def kernel(
    ranks,
    parts,
    strong,
    sar_hbm,
    places,
    turns,
    matrices_hbm,
    twist_hbm,
    image_hbm,
    phase_out,
    sar,
    matrices,
    ahead_left,
    back_right,
    ahead_right,
    back_left,
    twist,
    plain,
    stage,
    rows,
    hist,
    sums,
    phase,
    near_in,
    far_in,
    grads,
    ready,
    landed,
    image,
    load_sem,
    image_sem,
    in_send,
    in_recv,
    near_send,
    near_recv,
    far_send,
    far_recv,
    grad_send,
    grad_recv,
    out_send,
    out_recv,
):
    devices = ranks * parts
    near = near_in.shape[1]
    far = far_in.shape[1]
    block = SIDE // near
    rank = lax.axis_index("rng")
    part = lax.axis_index("az")
    me = rank * parts + part
    lines = rows.shape[1]
    units = hist.shape[0]
    unit = lines // units
    bins = stage.shape[1]
    depth = stage.shape[2]
    mine_strong = strong // parts
    mine_other = lines - mine_strong
    strong_units = mine_strong // unit
    groups = bins // 8
    slot_at, bin_at, shift_at, width_at = 0, bins, 2 * bins, 2 * bins + strong

    loads = [
        pltpu.make_async_copy(source, target, load_sem.at[at])
        for at, (source, target) in enumerate(
            [
                (sar_hbm, sar),
                (matrices_hbm, matrices),
                (twist_hbm, twist),
            ]
        )
    ]
    loads[0].start()

    barrier = pltpu.get_barrier_semaphore()

    def at_device(other):
        return (other // parts, other % parts)

    group_near, place_near = me // near, me % near

    def near_device(place):
        return group_near * near + place

    def far_device(group):
        return group * near + place_near

    greeted = [near_device((place_near + step) % near) for step in range(1, near)]
    if far <= 8:
        greeted += [far_device((group_near + step) % far) for step in range(1, far)]
    if parts > near or near % parts:
        greeted += [rank * parts + (part + step) % parts for step in range(1, parts)]
    for other in greeted:
        pl.semaphore_signal(barrier, inc=1, device_id=at_device(other), device_id_type=MESH)
    awaited = len(greeted)
    if far > 8:
        awaited += far - 1

        @pl.loop(1, far)
        def _(step):
            other = far_device((group_near + step) % far)
            pl.semaphore_signal(barrier, inc=1, device_id=at_device(other), device_id_type=MESH)

    for load in loads[1:]:
        load.start()
    loads[0].wait()

    for half in range(2):

        @pl.loop(0, groups)
        def _(group):
            spot = pl.ds(pl.multiple_of(group * 8, 8), 8)
            plain[half, spot] = sar[half, spot, :].reshape(8, depth, SIDE)

    def arrange(first, last):
        @pl.loop(first, last)
        def _(slot):
            source = places[bin_at + slot]
            for half in range(2):
                stage[half, slot] = plain[half, source]

    arrange(0, strong)
    pl.semaphore_wait(barrier, awaited)

    mine = pl.ds(pl.multiple_of(part * depth, depth), depth)

    def strong_slot(pair, owner):
        return mine_strong * owner + unit * pair

    def other_slot(pair, owner):
        return strong + mine_other * owner + unit * (pair - strong_units)

    def bring(slot_of, pair, source, target):
        return pltpu.make_async_remote_copy(
            src_ref=stage.at[:, pl.ds(slot_of(pair, target), unit)],
            dst_ref=rows.at[:, pl.ds(unit * pair, unit), pl.ds(pl.multiple_of(source * depth, depth), depth)],
            send_sem=in_send.at[pair, target],
            recv_sem=in_recv.at[pair, source],
            device_id=(rank, target),
            device_id_type=MESH,
        )

    order = sorted(range(1, parts), key=lambda step: abs(step - parts // 2))

    def begin(slot_of, pair):
        for step in order:
            bring(slot_of, pair, part, (part + step) % parts).start()

    def arrived(slot_of, pair):
        for step in order:
            other = (part + step) % parts
            bring(slot_of, pair, other, other).wait_recv()

    @pl.loop(0, strong_units)
    def _(pair):
        begin(strong_slot, pair)

    arrange(strong, bins)
    for half in range(2):

        @pl.loop(0, mine_strong)
        def _(line):
            rows[half, line, mine, :] = stage[half, mine_strong * part + line]

        @pl.loop(0, mine_other)
        def _(line):
            rows[half, mine_strong + line, mine, :] = stage[half, strong + mine_other * part + line]

    sums[...] = jnp.zeros_like(sums)
    cells = (
        lax.broadcasted_iota(jnp.int32, (SIDE, SIDE), 0) * SIDE
        + lax.broadcasted_iota(jnp.int32, (SIDE, SIDE), 1)
    )
    for load in loads[1:]:
        load.wait()
    ahead_h, ahead_l = halves(matrices[0])
    back_h, back_l = halves(matrices[1])
    ahead_left[...] = jnp.concatenate([ahead_h, ahead_l, ahead_h], axis=1)
    back_right[...] = jnp.concatenate([back_h, back_h, back_l], axis=0)
    ahead_right[...] = jnp.concatenate([ahead_h, ahead_h, ahead_l], axis=0)
    back_left[...] = jnp.concatenate([back_h, back_l, back_h], axis=1)

    def add_terms(turn, pair, value):
        masks = []
        for line in range(unit):
            at = mine_strong * part + pair * unit + line
            width = places[width_at + at]
            offset = (cells - (places[shift_at + at] - width // 2)) & (SIDE * SIDE - 1)
            masks.append((offset < width).astype(jnp.float32))
        mask = jnp.concatenate(masks, axis=1)
        mask = jnp.concatenate([mask, mask], axis=0)
        spectra = forward(value * mask, ahead_left, back_right, twist)
        num = sums[turn, 0]
        den = sums[turn, 1]
        for line in range(unit):
            at = mine_strong * part + pair * unit + line
            cos_h, cos_l, sin_h, sin_l = line_turn(turns, places[shift_at + at])
            spec_r = spectra[line * SIDE : (line + 1) * SIDE, :SIDE]
            spec_i = spectra[line * SIDE : (line + 1) * SIDE, SIDE:]
            prev_r, prev_i = previous(spec_r), previous(spec_i)
            cross_i = prev_r * spec_i - prev_i * spec_r
            cross_r = prev_r * spec_r + prev_i * spec_i
            rest = cross_i * cos_l + cross_r * sin_l
            num = num + ((cross_i * cos_h + cross_r * sin_h) + rest)
            den = den + (spec_r * spec_r + spec_i * spec_i)
        sums[turn, 0] = num
        sums[turn, 1] = den

    def gathered(pair):
        return jnp.concatenate(
            [
                jnp.concatenate([rows[half, pair * unit + at] for at in range(unit)], axis=1)
                for half in range(2)
            ],
            axis=0,
        )

    @pl.loop(0, strong_units)
    def _(pair):
        arrived(strong_slot, pair)
        if units == 2 * strong_units:
            begin(other_slot, strong_units + pair)
        add_terms(0, pair, gathered(pair))

    if units != 2 * strong_units:

        @pl.loop(strong_units, units)
        def _(pair):
            begin(other_slot, pair)

    def add_history(first, last, slot_of=None):
        @pl.loop(first, last)
        def _(pair):
            if slot_of is not None:
                arrived(slot_of, pair)
            hist[pair] = forward(gathered(pair), ahead_left, back_right, twist)

    row_ids = lax.broadcasted_iota(jnp.int32, (SIDE, SIDE), 0)
    col_ids = lax.broadcasted_iota(jnp.int32, (SIDE, SIDE), 1)
    block_rows = lax.broadcasted_iota(jnp.int32, (block, SIDE), 0)
    block_cols = lax.broadcasted_iota(jnp.int32, (block, SIDE), 1)

    def near_spot(place):
        return pl.ds(pl.multiple_of(place * block, block), block)

    def give(turn, source, target):
        return pltpu.make_async_remote_copy(
            src_ref=sums.at[turn, :, near_spot(target)],
            dst_ref=near_in.at[turn, source],
            send_sem=near_send.at[turn, target],
            recv_sem=near_recv.at[turn, source],
            device_id=at_device(near_device(target)),
            device_id_type=MESH,
        )

    def spread(turn, source, target):
        return pltpu.make_async_remote_copy(
            src_ref=far_in.at[turn, source],
            dst_ref=far_in.at[turn, source],
            send_sem=far_send.at[turn, target],
            recv_sem=far_recv.at[turn, source],
            device_id=at_device(far_device(target)),
            device_id_type=MESH,
        )

    def share(turn, source, target):
        return pltpu.make_async_remote_copy(
            src_ref=grads.at[turn, near_spot(source)],
            dst_ref=grads.at[turn, near_spot(source)],
            send_sem=grad_send.at[turn, target],
            recv_sem=grad_recv.at[turn, source],
            device_id=at_device(near_device(target)),
            device_id_type=MESH,
        )

    def others(own, count, act):
        if count <= 8:
            for step in range(1, count):
                act((own + step) % count)
        else:

            @pl.loop(1, count)
            def _(step):
                act((own + step) % count)

    def reduce_sums(turn, first_task, second_task):
        others(place_near, near, lambda place: give(turn, place_near, place).start())
        first_task()
        total = sums[turn, :, near_spot(place_near), :]
        for step in range(1, near):
            place = (place_near + step) % near
            give(turn, place, place).wait_recv()
            total = total + near_in[turn, place]
        far_in[turn, group_near] = total
        others(group_near, far, lambda group: spread(turn, group_near, group).start())
        second_task()
        others(group_near, far, lambda group: spread(turn, group, group).wait_recv())
        total = far_in[turn, 0]
        if far <= 8:
            for group in range(1, far):
                total = total + far_in[turn, group]
        else:
            total = lax.fori_loop(1, far, lambda group, value: value + far_in[turn, group], total)
        no_first = (block_rows == 0) & (block_cols == 0) & (place_near == 0)
        grads[turn, near_spot(place_near), :] = jnp.where(
            no_first, 0.0, total[0] / (total[1] + epsilon)
        )
        others(place_near, near, lambda place: share(turn, place_near, place).start())
        others(place_near, near, lambda place: share(turn, place, place).wait_recv())
        gradient = grads[turn]
        lower = (row_ids >= col_ids).astype(jnp.float32)
        upper = (row_ids < col_ids).astype(jnp.float32)
        inside = jnp.dot(
            lower, gradient, precision=lax.Precision.HIGHEST, preferred_element_type=jnp.float32
        )
        columns = jnp.broadcast_to(inside[SIDE - 1 :], (8, SIDE))
        before = jnp.dot(
            columns, upper, precision=lax.Precision.HIGHEST, preferred_element_type=jnp.float32
        )
        running = inside + before[:1]
        phase[...] = running if turn == 0 else phase[...] + running

    def drain(turn):
        others(place_near, near, lambda place: give(turn, place_near, place).wait_send())
        others(group_near, far, lambda group: spread(turn, group_near, group).wait_send())
        others(place_near, near, lambda place: share(turn, place_near, place).wait_send())

    def nothing():
        pass

    middle = strong_units // 2
    halfway = strong_units + (units - strong_units) // 2
    for turn in range(ITERS):
        if turn > 0:
            cosine, sine = jnp.cos(phase[...]), jnp.sin(phase[...])

            @pl.loop(0, strong_units)
            def _(pair):
                value = inverse(correct(hist[pair], cosine, sine), ahead_right, back_left, twist)
                add_terms(turn, pair, value)

        first_task, second_task = nothing, nothing
        if turn == 0:
            first_task = lambda: add_history(0, middle)
            second_task = lambda: add_history(middle, strong_units)
        elif turn == ITERS - 1:
            first_task = lambda: add_history(strong_units, halfway, other_slot)
            second_task = lambda: add_history(halfway, units, other_slot)
        reduce_sums(turn, first_task, second_task)

    cosine, sine = jnp.cos(phase[...]), jnp.sin(phase[...])

    def send_out(slot_of, pair, source, target):
        return pltpu.make_async_remote_copy(
            src_ref=ready.at[:, pl.ds(unit * pair, unit), pl.ds(pl.multiple_of(target * depth, depth), depth)],
            dst_ref=landed.at[:, pl.ds(slot_of(pair, source), unit)],
            send_sem=out_send.at[pair, target],
            recv_sem=out_recv.at[pair, source],
            device_id=(rank, target),
            device_id_type=MESH,
        )

    kinds = ((0, strong_units, strong_slot), (strong_units, units, other_slot))
    for first, last, slot_of in kinds:

        @pl.loop(first, last)
        def _(pair):
            value = inverse(correct(hist[pair], cosine, sine), ahead_right, back_left, twist)
            for half in range(2):
                for line in range(unit):
                    ready[half, unit * pair + line] = value[
                        half * SIDE : (half + 1) * SIDE, line * SIDE : (line + 1) * SIDE
                    ]
            for step in order:
                send_out(slot_of, pair, part, (part + step) % parts).start()
            for half in range(2):
                for line in range(unit):
                    landed[half, slot_of(pair, part) + line] = ready[
                        half, unit * pair + line, mine, :
                    ]

    for turn in range(ITERS):
        drain(turn)
    plain[0, : SIDE // depth] = phase[...].T.reshape(SIDE // depth, depth, SIDE)
    phase_out[...] = plain[0, part]

    for first, last, slot_of in kinds:

        @pl.loop(first, last)
        def _(pair):
            for step in order:
                bring(slot_of, pair, part, (part + step) % parts).wait_send()
            for step in order:
                other = (part + step) % parts
                send_out(slot_of, pair, other, other).wait_recv()

    def write(half, group):
        spot = pl.ds(pl.multiple_of(group * 8, 8), 8)
        return pltpu.make_async_copy(
            image.at[half, spot], image_hbm.at[half, spot], image_sem.at[half, group]
        )

    for half in range(2):

        @pl.loop(0, groups)
        def _(group):
            found = [landed[half, places[slot_at + group * 8 + at]] for at in range(8)]
            spot = pl.ds(pl.multiple_of(group * 8, 8), 8)
            image[half, spot, :] = jnp.stack(found).reshape(8, depth * SIDE)
            write(half, group).start()

    for first, last, slot_of in kinds:

        @pl.loop(first, last)
        def _(pair):
            for step in order:
                send_out(slot_of, pair, part, (part + step) % parts).wait_send()

    for half in range(2):

        @pl.loop(0, groups)
        def _(group):
            write(half, group).wait()


def local(ranks, parts, sar_image, strong_index, shifts, widths):
    bins = sar_image.shape[1]
    here = sar_image.shape[2]
    depth = here // SIDE
    lines = bins // parts
    strong = strong_index.shape[0]
    devices = ranks * parts
    unit = min(4, strong // parts)
    units = lines // unit
    near = 8
    far = devices // near
    chosen = strong_index % bins
    ids = jnp.arange(bins, dtype=jnp.int32)
    same = chosen[None, :] == ids[:, None]
    ahead = (chosen[None, :] < ids[:, None]).astype(jnp.int32)
    order = jnp.arange(strong, dtype=jnp.int32)[None, :]
    is_strong = jnp.any(same, axis=1)
    slots = jnp.where(
        is_strong,
        jnp.sum(jnp.where(same, order, 0), axis=1),
        strong + ids - jnp.sum(ahead, axis=1),
    )
    located = jnp.sum(jnp.where(slots[None, :] == ids[:, None], ids[None, :], 0), axis=1)
    places = jnp.concatenate([slots, located, shifts, widths])
    tables = make_tables(unit)
    vmem = pl.BlockSpec(memory_space=pltpu.VMEM)
    smem = pl.BlockSpec(memory_space=pltpu.SMEM)
    anywhere = pl.BlockSpec(memory_space=pltpu.HBM)
    dma = pltpu.SemaphoreType.DMA
    image, phase = pl.pallas_call(
        functools.partial(kernel, ranks, parts, strong),
        out_shape=(
            jax.ShapeDtypeStruct((2, bins, here), jnp.float32),
            jax.ShapeDtypeStruct((depth, SIDE), jnp.float32),
        ),
        in_specs=[anywhere, smem, smem] + [anywhere] * 2,
        out_specs=(anywhere, vmem),
        scratch_shapes=[
            pltpu.VMEM((2, bins, here), jnp.float32),
            pltpu.VMEM(tables[0].shape, jnp.float32),
            pltpu.VMEM((2 * SIDE, 6 * SIDE), jnp.bfloat16),
            pltpu.VMEM((6 * SIDE, 2 * SIDE), jnp.bfloat16),
            pltpu.VMEM((6 * SIDE, 2 * SIDE), jnp.bfloat16),
            pltpu.VMEM((2 * SIDE, 6 * SIDE), jnp.bfloat16),
            pltpu.VMEM(tables[1].shape, jnp.float32),
            pltpu.VMEM((2, bins, depth, SIDE), jnp.float32),
            pltpu.VMEM((2, bins, depth, SIDE), jnp.float32),
            pltpu.VMEM((2, lines, SIDE, SIDE), jnp.float32),
            pltpu.VMEM((units, unit * SIDE, 2 * SIDE), jnp.float32),
            pltpu.VMEM((ITERS, 2, SIDE, SIDE), jnp.float32),
            pltpu.VMEM((SIDE, SIDE), jnp.float32),
            pltpu.VMEM((ITERS, near, 2, SIDE // near, SIDE), jnp.float32),
            pltpu.VMEM((ITERS, far, 2, SIDE // near, SIDE), jnp.float32),
            pltpu.VMEM((ITERS, SIDE, SIDE), jnp.float32),
            pltpu.VMEM((2, lines, SIDE, SIDE), jnp.float32),
            pltpu.VMEM((2, bins, depth, SIDE), jnp.float32),
            pltpu.VMEM((2, bins, here), jnp.float32),
            dma((3,)),
            dma((2, bins // 8)),
            dma((units, parts)),
            dma((units, parts)),
            dma((ITERS, near)),
            dma((ITERS, near)),
            dma((ITERS, far)),
            dma((ITERS, far)),
            dma((ITERS, near)),
            dma((ITERS, near)),
            dma((units, parts)),
            dma((units, parts)),
        ],
        compiler_params=pltpu.CompilerParams(
            collective_id=0, has_side_effects=True, vmem_limit_bytes=56 * 2**20
        ),
        name="autofocus",
    )(sar_image, places, jnp.asarray(make_turns()), *[jnp.asarray(t) for t in tables])
    return image, phase.reshape(here)


def solution(mesh):
    placed = (P(None, "rng", "az"), P("rng"), P("rng"), P("rng"))
    return jax.shard_map(
        functools.partial(local, mesh.shape["rng"], mesh.shape["az"]),
        mesh=mesh,
        in_specs=placed,
        out_specs=(P(None, "rng", "az"), P("az")),
        check_vma=False,
    )
```

time: 102 us -> 89.7 us (0.88)
  Pallas kernels: 90.3 us -> 82.8 us
  local copies, waits for them, and re-layouts: 9.14 us -> 3.73 us
    pallas_call x1, Pallas kernels: 90.3 us -> 82.8 us  [local(): pl.pallas_call(functools.partial(kernel, ranks, parts, strong), out_shape...]
    unnamed x16 -> x4, local copies, waits for them, and re-layouts: 9.14 us -> 3.73 us
where the time goes in v2:
time: 89.7 us; the launch traced here: 89.4 us
  Pallas kernels  82.8 us (92%)
  local copies, waits for them, and re-layouts  3.73 us (4%)
  other arithmetic  2.28 us (3%)
    pallas_call x1, Pallas kernels, local(): pl.pallas_call(functools.partial(kernel, ranks, parts, strong), out_shape...  82.8 us
    unnamed x4, local copies, waits for them, and re-layouts  3.73 us

profile of v2, /device:TPU:0, one launch (start us, length us, event | category | flops | bytes accessed | tf_op | source)
XLA Modules:
  0.0 89.4 jit_solution(14961404601683474479)
XLA Ops:
  0.6 0.7 and_select_fusion
  1.3 0.1 fusion
  1.4 0.1 convert_reduce_fusion
  1.5 0.1 select_reduce_fusion
  1.6 1.3 %pad_add_fusion.places = s32[192]{0:T(256)} fusion(s32[32]{0:T(128)} %param.10, s32[32]{0:T(128)} %param.9, s32[64]{0:T(128)S(1)} %select_reduce_fusion, s32[64]{0:T(128)S(1)} %subtract_select_fusion), kind=kLoop, calls=%fused_computation.10 | loop fusion | flops 576 | bytes 1536 | tf_op jit(solution)/shard_map/concatenate | solution.py:573
  2.9 82.8 %autofocus.1 = (f32[2,64,4096]{2,1,0:T(8,128)}, f32[32,128]{1,0:T(8,128)}) custom-call(f32[2,64,4096]{2,1,0:T(8,128)} %sar_hbm.1, s32[192]{0:T(256)} %pad_add_fusion.places, f32[1024]{0:T(1024)} %constant.26.clone.turns, f32[2,256,256]{2,1,0:T(8,128)} %constant.27.clone.matrices_hbm, f32[2,128,512]{2,1,0:T(8,128)} %constant.28.clone.twist_hbm), custom_call_target="tpu_custom_call" | custom-call | tf_op jit(solution)/shard_map/autofocus/pallas_call | solution.py:579
  85.7 0.0 copy-start
  85.7 3.1 %copy.11 = f32[2,64,4096]{2,1,0:T(8,128)} copy(f32[2,64,4096]{2,1,0:T(8,128)} %get-tuple-element.10) | data formatting | bytes 4194304
  88.8 0.0 copy-done
  88.8 0.6 copy.12
  (1 shorter events, 0.0 us)
Async XLA Ops:
  85.7 3.1 %copy-start = (f32[32,128]{1,0:T(8,128)S(1)}, f32[32,128]{1,0:T(8,128)}, u32[]{:S(2)}) copy-start(f32[32,128]{1,0:T(8,128)} %get-tuple-element.5) | copy-start | bytes 49156

commit v3 on v2

--- a/solution.py
+++ b/solution.py
@@ -132,7 +132,7 @@
     turns,
     matrices_hbm,
     twist_hbm,
-    image_hbm,
+    landed,
     phase_out,
     sar,
     matrices,
@@ -142,6 +142,7 @@
     back_left,
     twist,
     plain,
+    natural,
     stage,
     rows,
     hist,
@@ -151,10 +152,8 @@
     far_in,
     grads,
     ready,
-    landed,
-    image,
     load_sem,
-    image_sem,
+    own_sem,
     in_send,
     in_recv,
     near_send,
@@ -234,14 +233,20 @@
         @pl.loop(0, groups)
         def _(group):
             spot = pl.ds(pl.multiple_of(group * 8, 8), 8)
-            plain[half, spot] = sar[half, spot, :].reshape(8, depth, SIDE)
+            for cut in range(depth):
+                plain[pl.ds((half * bins + group * 8) * depth + cut, 8, stride=depth), :] = sar[
+                    half, spot, cut * SIDE : (cut + 1) * SIDE
+                ]
+            for at in range(8):
+                start = pl.multiple_of((half * bins + group * 8 + at) * depth, depth)
+                natural[half, group * 8 + at] = plain[pl.ds(start, depth), :]
 
     def arrange(first, last):
         @pl.loop(first, last)
         def _(slot):
             source = places[bin_at + slot]
             for half in range(2):
-                stage[half, slot] = plain[half, source]
+                stage[half, slot] = natural[half, source]
 
     arrange(0, strong)
     pl.semaphore_wait(barrier, awaited)
@@ -484,6 +489,13 @@
             device_id_type=MESH,
         )
 
+    def keep(slot_of, pair):
+        return pltpu.make_async_copy(
+            ready.at[:, pl.ds(unit * pair, unit), mine],
+            landed.at[:, pl.ds(slot_of(pair, part), unit)],
+            own_sem.at[pair],
+        )
+
     kinds = ((0, strong_units, strong_slot), (strong_units, units, other_slot))
     for first, last, slot_of in kinds:
 
@@ -497,16 +509,13 @@
                     ]
             for step in order:
                 send_out(slot_of, pair, part, (part + step) % parts).start()
-            for half in range(2):
-                for line in range(unit):
-                    landed[half, slot_of(pair, part) + line] = ready[
-                        half, unit * pair + line, mine, :
-                    ]
+            keep(slot_of, pair).start()
 
     for turn in range(ITERS):
         drain(turn)
-    plain[0, : SIDE // depth] = phase[...].T.reshape(SIDE // depth, depth, SIDE)
-    phase_out[...] = plain[0, part]
+    turned = phase[...].T
+    plain[:SIDE, :] = turned
+    phase_out[...] = plain[mine, :]
 
     for first, last, slot_of in kinds:
 
@@ -517,6 +526,22 @@
             for step in order:
                 other = (part + step) % parts
                 send_out(slot_of, pair, other, other).wait_recv()
+                send_out(slot_of, pair, part, other).wait_send()
+            keep(slot_of, pair).wait()
+
+def place_rows(
+    landed_hbm, places, phase, image_hbm, phase_out, landed, plain, image, load_sem, image_sem
+):
+    bins = landed.shape[1]
+    depth = landed.shape[2]
+    groups = bins // 8
+    loads = [
+        pltpu.make_async_copy(landed_hbm.at[half], landed.at[half], load_sem.at[half])
+        for half in range(2)
+    ]
+    for load in loads:
+        load.start()
+    phase_out[...] = phase[...]
 
     def write(half, group):
         spot = pl.ds(pl.multiple_of(group * 8, 8), 8)
@@ -525,20 +550,21 @@
         )
 
     for half in range(2):
+        loads[half].wait()
 
         @pl.loop(0, groups)
         def _(group):
-            found = [landed[half, places[slot_at + group * 8 + at]] for at in range(8)]
+            base = (half * bins + group * 8) * depth
+            for at in range(8):
+                plain[pl.ds(pl.multiple_of(base + at * depth, depth), depth), :] = landed[
+                    half, places[group * 8 + at]
+                ]
             spot = pl.ds(pl.multiple_of(group * 8, 8), 8)
-            image[half, spot, :] = jnp.stack(found).reshape(8, depth * SIDE)
+            for cut in range(depth):
+                image[half, spot, cut * SIDE : (cut + 1) * SIDE] = plain[
+                    pl.ds(base + cut, 8, stride=depth), :
+                ]
             write(half, group).start()
-
-    for first, last, slot_of in kinds:
-
-        @pl.loop(first, last)
-        def _(pair):
-            for step in order:
-                send_out(slot_of, pair, part, (part + step) % parts).wait_send()
 
     for half in range(2):
 
@@ -576,10 +602,10 @@
     smem = pl.BlockSpec(memory_space=pltpu.SMEM)
     anywhere = pl.BlockSpec(memory_space=pltpu.HBM)
     dma = pltpu.SemaphoreType.DMA
-    image, phase = pl.pallas_call(
+    landed, phase = pl.pallas_call(
         functools.partial(kernel, ranks, parts, strong),
         out_shape=(
-            jax.ShapeDtypeStruct((2, bins, here), jnp.float32),
+            jax.ShapeDtypeStruct((2, bins, depth, SIDE), jnp.float32),
             jax.ShapeDtypeStruct((depth, SIDE), jnp.float32),
         ),
         in_specs=[anywhere, smem, smem] + [anywhere] * 2,
@@ -592,6 +618,7 @@
             pltpu.VMEM((6 * SIDE, 2 * SIDE), jnp.bfloat16),
             pltpu.VMEM((2 * SIDE, 6 * SIDE), jnp.bfloat16),
             pltpu.VMEM(tables[1].shape, jnp.float32),
+            pltpu.VMEM((2 * bins * depth, SIDE), jnp.float32),
             pltpu.VMEM((2, bins, depth, SIDE), jnp.float32),
             pltpu.VMEM((2, bins, depth, SIDE), jnp.float32),
             pltpu.VMEM((2, lines, SIDE, SIDE), jnp.float32),
@@ -602,10 +629,8 @@
             pltpu.VMEM((ITERS, far, 2, SIDE // near, SIDE), jnp.float32),
             pltpu.VMEM((ITERS, SIDE, SIDE), jnp.float32),
             pltpu.VMEM((2, lines, SIDE, SIDE), jnp.float32),
-            pltpu.VMEM((2, bins, depth, SIDE), jnp.float32),
-            pltpu.VMEM((2, bins, here), jnp.float32),
             dma((3,)),
-            dma((2, bins // 8)),
+            dma((units,)),
             dma((units, parts)),
             dma((units, parts)),
             dma((ITERS, near)),
@@ -622,6 +647,24 @@
         ),
         name="autofocus",
     )(sar_image, places, jnp.asarray(make_turns()), *[jnp.asarray(t) for t in tables])
+    image, phase = pl.pallas_call(
+        place_rows,
+        out_shape=(
+            jax.ShapeDtypeStruct((2, bins, here), jnp.float32),
+            jax.ShapeDtypeStruct((depth, SIDE), jnp.float32),
+        ),
+        in_specs=[anywhere, smem, vmem],
+        out_specs=(anywhere, vmem),
+        scratch_shapes=[
+            pltpu.VMEM((2, bins, depth, SIDE), jnp.float32),
+            pltpu.VMEM((2 * bins * depth, SIDE), jnp.float32),
+            pltpu.VMEM((2, bins, here), jnp.float32),
+            dma((2,)),
+            dma((2, bins // 8)),
+        ],
+        compiler_params=pltpu.CompilerParams(vmem_limit_bytes=56 * 2**20),
+        name="place_rows",
+    )(landed, places, phase)
     return image, phase.reshape(here)
 
 

time: 89.7 us -> 90.1 us (level)
  Pallas kernels: 82.8 us -> 86.8 us
  local copies, waits for them, and re-layouts: 3.73 us -> 0 us
    pallas_call x0 -> x1, Pallas kernels: none -> 4.88 us  [local(): pl.pallas_call(place_rows, out_shape=(jax.ShapeDtypeStruct((2, bins, here...]
    unnamed x4 -> x0, local copies, waits for them, and re-layouts: 3.73 us -> none
where the time goes in v3:
time: 90.1 us; the launch traced here: 89.8 us
  Pallas kernels  86.8 us (96%)
  other arithmetic  2.3 us (3%)
    pallas_call x1, Pallas kernels, local(): pl.pallas_call(functools.partial(kernel, ranks, parts, strong), out_shape...  82 us
    pallas_call x1, Pallas kernels, local(): pl.pallas_call(place_rows, out_shape=(jax.ShapeDtypeStruct((2, bins, here...  4.88 us

profile of v3, /device:TPU:0, one launch (start us, length us, event | category | flops | bytes accessed | tf_op | source)
XLA Modules:
  0.0 89.8 jit_solution(2932336269634124801)
XLA Ops:
  0.6 0.7 and_select_fusion
  1.3 0.1 fusion
  1.4 0.1 convert_reduce_fusion
  1.5 0.1 select_reduce_fusion
  1.6 1.3 %pad_add_fusion.places = s32[192]{0:T(256)} fusion(s32[32]{0:T(128)} %param.10, s32[32]{0:T(128)} %param.9, s32[64]{0:T(128)S(1)} %select_reduce_fusion, s32[64]{0:T(128)S(1)} %subtract_select_fusion), kind=kLoop, calls=%fused_computation.10 | loop fusion | flops 576 | bytes 1536 | tf_op jit(solution)/shard_map/concatenate | solution.py:599
  2.9 82.0 %autofocus.1 = (f32[2,64,32,128]{3,2,1,0:T(8,128)}, f32[32,128]{1,0:T(8,128)}) custom-call(f32[2,64,4096]{2,1,0:T(8,128)} %sar_hbm.1, s32[192]{0:T(256)} %pad_add_fusion.places, f32[1024]{0:T(1024)} %constant.26.clone.turns, f32[2,256,256]{2,1,0:T(8,128)} %constant.27.clone.matrices_hbm, f32[2,128,512]{2,1,0:T(8,128)} %constant.28.clone.twist_hbm), custom_call_target="tpu_custom_call" | custom-call | tf_op jit(solution)/shard_map/autofocus/pallas_call | solution.py:605
  84.9 4.9 %place_rows.1 = (f32[2,64,4096]{2,1,0:T(8,128)}, f32[32,128]{1,0:T(8,128)}) custom-call(f32[2,64,32,128]{3,2,1,0:T(8,128)} %get-tuple-element.6.landed_hbm, s32[192]{0:T(256)} %pad_add_fusion.places, f32[32,128]{1,0:T(8,128)} %get-tuple-element.7.phase), custom_call_target="tpu_custom_call" | custom-call | tf_op jit(solution)/shard_map/place_rows/pallas_call | solution.py:650
  (1 shorter events, 0.0 us)

commit v4 on v3

--- a/solution.py
+++ b/solution.py
@@ -140,6 +140,7 @@
     back_right,
     ahead_right,
     back_left,
+    back_part,
     twist,
     plain,
     natural,
@@ -152,6 +153,7 @@
     far_in,
     grads,
     ready,
+    prepared,
     load_sem,
     own_sem,
     in_send,
@@ -164,6 +166,8 @@
     grad_recv,
     out_send,
     out_recv,
+    pass_send,
+    pass_recv,
 ):
     devices = ranks * parts
     near = near_in.shape[1]
@@ -177,9 +181,13 @@
     unit = lines // units
     bins = stage.shape[1]
     depth = stage.shape[2]
+    core = part % 2
+    twin = part + 1 - 2 * core
+    wide = 2 * depth
     mine_strong = strong // parts
     mine_other = lines - mine_strong
     strong_units = mine_strong // unit
+    ratio = (units - strong_units) // strong_units
     groups = bins // 8
     slot_at, bin_at, shift_at, width_at = 0, bins, 2 * bins, 2 * bins + strong
 
@@ -257,7 +265,7 @@
         return mine_strong * owner + unit * pair
 
     def other_slot(pair, owner):
-        return strong + mine_other * owner + unit * (pair - strong_units)
+        return strong + mine_other * (owner % 2) + unit * (pair - strong_units)
 
     def bring(slot_of, pair, source, target):
         return pltpu.make_async_remote_copy(
@@ -293,7 +301,7 @@
 
         @pl.loop(0, mine_other)
         def _(line):
-            rows[half, mine_strong + line, mine, :] = stage[half, strong + mine_other * part + line]
+            rows[half, mine_strong + line, mine, :] = stage[half, strong + mine_other * core + line]
 
     sums[...] = jnp.zeros_like(sums)
     cells = (
@@ -308,6 +316,17 @@
     back_right[...] = jnp.concatenate([back_h, back_h, back_l], axis=0)
     ahead_right[...] = jnp.concatenate([ahead_h, ahead_h, ahead_l], axis=0)
     back_left[...] = jnp.concatenate([back_h, back_l, back_h], axis=1)
+    half_rows = pl.multiple_of((part // 2) * wide, wide)
+    part_h, part_l = halves(
+        jnp.concatenate(
+            [
+                matrices[1, pl.ds(half_rows, wide), :],
+                matrices[1, pl.ds(pl.multiple_of(SIDE + half_rows, wide), wide), :],
+            ],
+            axis=0,
+        )
+    )
+    back_part[...] = jnp.concatenate([part_h, part_l, part_h], axis=1)
 
     def add_terms(turn, pair, value):
         masks = []
@@ -347,15 +366,9 @@
     @pl.loop(0, strong_units)
     def _(pair):
         arrived(strong_slot, pair)
-        if units == 2 * strong_units:
-            begin(other_slot, strong_units + pair)
+        for at in range(ratio):
+            begin(other_slot, strong_units + pair * ratio + at)
         add_terms(0, pair, gathered(pair))
-
-    if units != 2 * strong_units:
-
-        @pl.loop(strong_units, units)
-        def _(pair):
-            begin(other_slot, pair)
 
     def add_history(first, last, slot_of=None):
         @pl.loop(first, last)
@@ -458,6 +471,7 @@
         pass
 
     middle = strong_units // 2
+    quarter = strong_units + (units - strong_units) // 4
     halfway = strong_units + (units - strong_units) // 2
     for turn in range(ITERS):
         if turn > 0:
@@ -473,8 +487,8 @@
             first_task = lambda: add_history(0, middle)
             second_task = lambda: add_history(middle, strong_units)
         elif turn == ITERS - 1:
-            first_task = lambda: add_history(strong_units, halfway, other_slot)
-            second_task = lambda: add_history(halfway, units, other_slot)
+            first_task = lambda: add_history(strong_units, quarter, other_slot)
+            second_task = lambda: add_history(quarter, halfway, other_slot)
         reduce_sums(turn, first_task, second_task)
 
     cosine, sine = jnp.cos(phase[...]), jnp.sin(phase[...])
@@ -496,20 +510,56 @@
             own_sem.at[pair],
         )
 
-    kinds = ((0, strong_units, strong_slot), (strong_units, units, other_slot))
-    for first, last, slot_of in kinds:
-
-        @pl.loop(first, last)
-        def _(pair):
-            value = inverse(correct(hist[pair], cosine, sine), ahead_right, back_left, twist)
-            for half in range(2):
-                for line in range(unit):
-                    ready[half, unit * pair + line] = value[
-                        half * SIDE : (half + 1) * SIDE, line * SIDE : (line + 1) * SIDE
-                    ]
-            for step in order:
-                send_out(slot_of, pair, part, (part + step) % parts).start()
-            keep(slot_of, pair).start()
+    @pl.loop(0, strong_units)
+    def _(pair):
+        value = inverse(correct(hist[pair], cosine, sine), ahead_right, back_left, twist)
+        for half in range(2):
+            for line in range(unit):
+                ready[half, unit * pair + line] = value[
+                    half * SIDE : (half + 1) * SIDE, line * SIDE : (line + 1) * SIDE
+                ]
+        for step in order:
+            send_out(strong_slot, pair, part, (part + step) % parts).start()
+        keep(strong_slot, pair).start()
+
+    def core_rows(which):
+        return pl.ds(pl.multiple_of(which * depth, depth), depth)
+
+    def pass_on(pair, source, target):
+        return pltpu.make_async_remote_copy(
+            src_ref=prepared.at[:, pl.ds(unit * (pair - strong_units), unit), core_rows(target % 2)],
+            dst_ref=landed.at[:, pl.ds(other_slot(pair, source), unit)],
+            send_sem=pass_send.at[pair - strong_units],
+            recv_sem=pass_recv.at[pair - strong_units],
+            device_id=(rank, target),
+            device_id_type=MESH,
+        )
+
+    def keep_other(pair):
+        return pltpu.make_async_copy(
+            prepared.at[:, pl.ds(unit * (pair - strong_units), unit), core_rows(core)],
+            landed.at[:, pl.ds(other_slot(pair, part), unit)],
+            own_sem.at[pair],
+        )
+
+    def finish_other(pair, spectra):
+        value = inverse(correct(spectra, cosine, sine), ahead_right, back_part, twist)
+        for half in range(2):
+            for line in range(unit):
+                prepared[half, unit * (pair - strong_units) + line] = value[
+                    half * wide : (half + 1) * wide, line * SIDE : (line + 1) * SIDE
+                ]
+        pass_on(pair, part, twin).start()
+        keep_other(pair).start()
+
+    @pl.loop(strong_units, halfway)
+    def _(pair):
+        finish_other(pair, hist[pair])
+
+    @pl.loop(halfway, units)
+    def _(pair):
+        arrived(other_slot, pair)
+        finish_other(pair, forward(gathered(pair), ahead_left, back_right, twist))
 
     for turn in range(ITERS):
         drain(turn)
@@ -517,17 +567,23 @@
     plain[:SIDE, :] = turned
     phase_out[...] = plain[mine, :]
 
-    for first, last, slot_of in kinds:
-
-        @pl.loop(first, last)
-        def _(pair):
-            for step in order:
-                bring(slot_of, pair, part, (part + step) % parts).wait_send()
-            for step in order:
-                other = (part + step) % parts
-                send_out(slot_of, pair, other, other).wait_recv()
-                send_out(slot_of, pair, part, other).wait_send()
-            keep(slot_of, pair).wait()
+    @pl.loop(strong_units, units)
+    def _(pair):
+        for step in order:
+            bring(other_slot, pair, part, (part + step) % parts).wait_send()
+        pass_on(pair, twin, twin).wait_recv()
+        pass_on(pair, part, twin).wait_send()
+        keep_other(pair).wait()
+
+    @pl.loop(0, strong_units)
+    def _(pair):
+        for step in order:
+            other = (part + step) % parts
+            bring(strong_slot, pair, part, other).wait_send()
+            send_out(strong_slot, pair, other, other).wait_recv()
+            send_out(strong_slot, pair, part, other).wait_send()
+        keep(strong_slot, pair).wait()
+
 
 def place_rows(
     landed_hbm, places, phase, image_hbm, phase_out, landed, plain, image, load_sem, image_sem
@@ -577,10 +633,12 @@
     bins = sar_image.shape[1]
     here = sar_image.shape[2]
     depth = here // SIDE
-    lines = bins // parts
     strong = strong_index.shape[0]
     devices = ranks * parts
     unit = min(4, strong // parts)
+    strong_lines = strong // parts
+    other_lines = (bins - strong) // 2
+    lines = strong_lines + other_lines
     units = lines // unit
     near = 8
     far = devices // near
@@ -617,6 +675,7 @@
             pltpu.VMEM((6 * SIDE, 2 * SIDE), jnp.bfloat16),
             pltpu.VMEM((6 * SIDE, 2 * SIDE), jnp.bfloat16),
             pltpu.VMEM((2 * SIDE, 6 * SIDE), jnp.bfloat16),
+            pltpu.VMEM((4 * depth, 6 * SIDE), jnp.bfloat16),
             pltpu.VMEM(tables[1].shape, jnp.float32),
             pltpu.VMEM((2 * bins * depth, SIDE), jnp.float32),
             pltpu.VMEM((2, bins, depth, SIDE), jnp.float32),
@@ -628,7 +687,8 @@
             pltpu.VMEM((ITERS, near, 2, SIDE // near, SIDE), jnp.float32),
             pltpu.VMEM((ITERS, far, 2, SIDE // near, SIDE), jnp.float32),
             pltpu.VMEM((ITERS, SIDE, SIDE), jnp.float32),
-            pltpu.VMEM((2, lines, SIDE, SIDE), jnp.float32),
+            pltpu.VMEM((2, strong_lines, SIDE, SIDE), jnp.float32),
+            pltpu.VMEM((2, other_lines, 2 * depth, SIDE), jnp.float32),
             dma((3,)),
             dma((units,)),
             dma((units, parts)),
@@ -641,6 +701,8 @@
             dma((ITERS, near)),
             dma((units, parts)),
             dma((units, parts)),
+            dma((other_lines // unit,)),
+            dma((other_lines // unit,)),
         ],
         compiler_params=pltpu.CompilerParams(
             collective_id=0, has_side_effects=True, vmem_limit_bytes=56 * 2**20

time: 90.1 us -> 90.5 us (level)
  no operation moved by 1% of the time
where the time goes in v4:
time: 90.5 us; the launch traced here: 90.2 us
  Pallas kernels  87.2 us (96%)
  other arithmetic  2.3 us (3%)
    pallas_call x1, Pallas kernels, local(): pl.pallas_call(functools.partial(kernel, ranks, parts, strong), out_shape...  82.3 us
    pallas_call x1, Pallas kernels, local(): pl.pallas_call(place_rows, out_shape=(jax.ShapeDtypeStruct((2, bins, here...  4.88 us

profile of v4, /device:TPU:0, one launch (start us, length us, event | category | flops | bytes accessed | tf_op | source)
XLA Modules:
  0.0 90.2 jit_solution(14540003407716444236)
XLA Ops:
  0.6 0.7 and_select_fusion
  1.3 0.1 fusion
  1.4 0.1 convert_reduce_fusion
  1.5 0.1 select_reduce_fusion
  1.6 1.3 %pad_add_fusion.places = s32[192]{0:T(256)} fusion(s32[32]{0:T(128)} %param.10, s32[32]{0:T(128)} %param.9, s32[64]{0:T(128)S(1)} %select_reduce_fusion, s32[64]{0:T(128)S(1)} %subtract_select_fusion), kind=kLoop, calls=%fused_computation.10 | loop fusion | flops 576 | bytes 1536 | tf_op jit(solution)/shard_map/concatenate | solution.py:657
  2.9 82.3 %autofocus.1 = (f32[2,64,32,128]{3,2,1,0:T(8,128)}, f32[32,128]{1,0:T(8,128)}) custom-call(f32[2,64,4096]{2,1,0:T(8,128)} %sar_hbm.1, s32[192]{0:T(256)} %pad_add_fusion.places, f32[1024]{0:T(1024)} %constant.26.clone.turns, f32[2,256,256]{2,1,0:T(8,128)} %constant.27.clone.matrices_hbm, f32[2,128,512]{2,1,0:T(8,128)} %constant.28.clone.twist_hbm), custom_call_target="tpu_custom_call" | custom-call | tf_op jit(solution)/shard_map/autofocus/pallas_call | solution.py:663
  85.3 4.9 %place_rows.1 = (f32[2,64,4096]{2,1,0:T(8,128)}, f32[32,128]{1,0:T(8,128)}) custom-call(f32[2,64,32,128]{3,2,1,0:T(8,128)} %get-tuple-element.6.landed_hbm, s32[192]{0:T(256)} %pad_add_fusion.places, f32[32,128]{1,0:T(8,128)} %get-tuple-element.7.phase), custom_call_target="tpu_custom_call" | custom-call | tf_op jit(solution)/shard_map/place_rows/pallas_call | solution.py:712
  (1 shorter events, 0.0 us)

commit v5 on v4

--- a/solution.py
+++ b/solution.py
@@ -477,7 +477,7 @@
         if turn > 0:
             cosine, sine = jnp.cos(phase[...]), jnp.sin(phase[...])
 
-            @pl.loop(0, strong_units)
+            @pl.loop(0, strong_units, unroll=True)
             def _(pair):
                 value = inverse(correct(hist[pair], cosine, sine), ahead_right, back_left, twist)
                 add_terms(turn, pair, value)
@@ -510,7 +510,7 @@
             own_sem.at[pair],
         )
 
-    @pl.loop(0, strong_units)
+    @pl.loop(0, strong_units, unroll=True)
     def _(pair):
         value = inverse(correct(hist[pair], cosine, sine), ahead_right, back_left, twist)
         for half in range(2):
@@ -518,6 +518,9 @@
                 ready[half, unit * pair + line] = value[
                     half * SIDE : (half + 1) * SIDE, line * SIDE : (line + 1) * SIDE
                 ]
+
+    @pl.loop(0, strong_units)
+    def _(pair):
         for step in order:
             send_out(strong_slot, pair, part, (part + step) % parts).start()
         keep(strong_slot, pair).start()
@@ -549,18 +552,28 @@
                 prepared[half, unit * (pair - strong_units) + line] = value[
                     half * wide : (half + 1) * wide, line * SIDE : (line + 1) * SIDE
                 ]
-        pass_on(pair, part, twin).start()
-        keep_other(pair).start()
-
-    @pl.loop(strong_units, halfway)
+
+    def deliver_others(first, last):
+        @pl.loop(first, last)
+        def _(pair):
+            pass_on(pair, part, twin).start()
+            keep_other(pair).start()
+
+    @pl.loop(strong_units, halfway, unroll=True)
     def _(pair):
         finish_other(pair, hist[pair])
 
+    deliver_others(strong_units, halfway)
+
     @pl.loop(halfway, units)
     def _(pair):
         arrived(other_slot, pair)
+
+    @pl.loop(halfway, units, unroll=True)
+    def _(pair):
         finish_other(pair, forward(gathered(pair), ahead_left, back_right, twist))
 
+    deliver_others(halfway, units)
     for turn in range(ITERS):
         drain(turn)
     turned = phase[...].T

time: 90.5 us -> 90.5 us (level)
  no operation moved by 1% of the time
where the time goes in v5:
time: 90.5 us; the launch traced here: 90.1 us
  Pallas kernels  87.2 us (96%)
  other arithmetic  2.3 us (3%)
    pallas_call x1, Pallas kernels, local(): pl.pallas_call(functools.partial(kernel, ranks, parts, strong), out_shape...  82.3 us
    pallas_call x1, Pallas kernels, local(): pl.pallas_call(place_rows, out_shape=(jax.ShapeDtypeStruct((2, bins, here...  4.88 us

profile of v5, /device:TPU:0, one launch (start us, length us, event | category | flops | bytes accessed | tf_op | source)
XLA Modules:
  0.0 90.1 jit_solution(8016089639297950933)
XLA Ops:
  0.6 0.7 and_select_fusion
  1.3 0.1 fusion
  1.4 0.1 convert_reduce_fusion
  1.5 0.1 select_reduce_fusion
  1.6 1.3 %pad_add_fusion.places = s32[192]{0:T(256)} fusion(s32[32]{0:T(128)} %param.10, s32[32]{0:T(128)} %param.9, s32[64]{0:T(128)S(1)} %select_reduce_fusion, s32[64]{0:T(128)S(1)} %subtract_select_fusion), kind=kLoop, calls=%fused_computation.10 | loop fusion | flops 576 | bytes 1536 | tf_op jit(solution)/shard_map/concatenate | solution.py:670
  2.9 82.3 %autofocus.1 = (f32[2,64,32,128]{3,2,1,0:T(8,128)}, f32[32,128]{1,0:T(8,128)}) custom-call(f32[2,64,4096]{2,1,0:T(8,128)} %sar_hbm.1, s32[192]{0:T(256)} %pad_add_fusion.places, f32[1024]{0:T(1024)} %constant.26.clone.turns, f32[2,256,256]{2,1,0:T(8,128)} %constant.27.clone.matrices_hbm, f32[2,128,512]{2,1,0:T(8,128)} %constant.28.clone.twist_hbm), custom_call_target="tpu_custom_call" | custom-call | tf_op jit(solution)/shard_map/autofocus/pallas_call | solution.py:676
  85.2 4.9 %place_rows.1 = (f32[2,64,4096]{2,1,0:T(8,128)}, f32[32,128]{1,0:T(8,128)}) custom-call(f32[2,64,32,128]{3,2,1,0:T(8,128)} %get-tuple-element.6.landed_hbm, s32[192]{0:T(256)} %pad_add_fusion.places, f32[32,128]{1,0:T(8,128)} %get-tuple-element.7.phase), custom_call_target="tpu_custom_call" | custom-call | tf_op jit(solution)/shard_map/place_rows/pallas_call | solution.py:725
  (1 shorter events, 0.0 us)

commit v6 on v2

--- a/solution.py
+++ b/solution.py
@@ -342,15 +342,7 @@
     @pl.loop(0, strong_units)
     def _(pair):
         arrived(strong_slot, pair)
-        if units == 2 * strong_units:
-            begin(other_slot, strong_units + pair)
         add_terms(0, pair, gathered(pair))
-
-    if units != 2 * strong_units:
-
-        @pl.loop(strong_units, units)
-        def _(pair):
-            begin(other_slot, pair)
 
     def add_history(first, last, slot_of=None):
         @pl.loop(first, last)
@@ -455,6 +447,12 @@
     middle = strong_units // 2
     halfway = strong_units + (units - strong_units) // 2
     for turn in range(ITERS):
+        if turn == 1:
+
+            @pl.loop(strong_units, units)
+            def _(pair):
+                begin(other_slot, pair)
+
         if turn > 0:
             cosine, sine = jnp.cos(phase[...]), jnp.sin(phase[...])
 

time: 89.7 us -> 88.2 us (0.983)
  Pallas kernels: 82.8 us -> 81.3 us
    pallas_call x1, Pallas kernels: 82.8 us -> 81.3 us  [local(): pl.pallas_call(functools.partial(kernel, ranks, parts, strong), out_shape...]
where the time goes in v6:
time: 88.2 us; the launch traced here: 88 us
  Pallas kernels  81.3 us (92%)
  local copies, waits for them, and re-layouts  3.73 us (4%)
  other arithmetic  2.28 us (3%)
    pallas_call x1, Pallas kernels, local(): pl.pallas_call(functools.partial(kernel, ranks, parts, strong), out_shape...  81.3 us
    unnamed x4, local copies, waits for them, and re-layouts  3.73 us

profile of v6, /device:TPU:0, one launch (start us, length us, event | category | flops | bytes accessed | tf_op | source)
XLA Modules:
  0.0 88.0 jit_solution(11338998326901563596)
XLA Ops:
  0.6 0.7 and_select_fusion
  1.3 0.1 fusion
  1.4 0.1 convert_reduce_fusion
  1.5 0.1 select_reduce_fusion
  1.6 1.3 %pad_add_fusion.places = s32[192]{0:T(256)} fusion(s32[32]{0:T(128)} %param.10, s32[32]{0:T(128)} %param.9, s32[64]{0:T(128)S(1)} %select_reduce_fusion, s32[64]{0:T(128)S(1)} %subtract_select_fusion), kind=kLoop, calls=%fused_computation.10 | loop fusion | flops 576 | bytes 1536 | tf_op jit(solution)/shard_map/concatenate | solution.py:571
  2.9 81.3 %autofocus.1 = (f32[2,64,4096]{2,1,0:T(8,128)}, f32[32,128]{1,0:T(8,128)}) custom-call(f32[2,64,4096]{2,1,0:T(8,128)} %sar_hbm.1, s32[192]{0:T(256)} %pad_add_fusion.places, f32[1024]{0:T(1024)} %constant.26.clone.turns, f32[2,256,256]{2,1,0:T(8,128)} %constant.27.clone.matrices_hbm, f32[2,128,512]{2,1,0:T(8,128)} %constant.28.clone.twist_hbm), custom_call_target="tpu_custom_call" | custom-call | tf_op jit(solution)/shard_map/autofocus/pallas_call | solution.py:577
  84.2 0.0 copy-start
  84.2 3.1 %copy.11 = f32[2,64,4096]{2,1,0:T(8,128)} copy(f32[2,64,4096]{2,1,0:T(8,128)} %get-tuple-element.10) | data formatting | bytes 4194304
  87.4 0.0 copy-done
  87.4 0.6 copy.12
  (1 shorter events, 0.0 us)
Async XLA Ops:
  84.2 3.1 %copy-start = (f32[32,128]{1,0:T(8,128)S(1)}, f32[32,128]{1,0:T(8,128)}, u32[]{:S(2)}) copy-start(f32[32,128]{1,0:T(8,128)} %get-tuple-element.5) | copy-start | bytes 49156
